TPU v7x, 128 devices: a whole 4x4x4 slice. The times are simulated.
128 devices in a mesh: section: 2 (over core), row: 4 (over x), col: 16 (over z, y).
Axes of the slice: x: 4, y: 4, z: 4, core: 2. Of those that a mesh axis runs over, the one named last changes fastest.
Arguments:
- pair_act: bfloat16 [2, 2, 256, 256, 128], P('section', None, 'row', 'col'), may hold values from -6 to 6
- pair_cot: float32 [2, 256, 256, 128], P(None, 'row', 'col'), may hold values from -6 to 6
- pad_mask: int32 [2, 256], replicated, may hold values 0 or 1
- ln_gain: float32 [2, 128], P('section'), may hold values from 0.25 to 1.75
- ln_bias: float32 [2, 128], P('section'), may hold values from -3 to 3
- proj_weight: bfloat16 [2, 128, 512], P('section'), may hold values from -0.5 to 0.5
- gate_weight: bfloat16 [2, 128, 128], P('section'), may hold values from -0.5 to 0.5
- out_gain: float32 [2, 128], P('section'), may hold values from 0.25 to 1.75
- out_bias: float32 [2, 128], P('section'), may hold values from -3 to 3
- out_weight: bfloat16 [2, 128, 128], P('section'), may hold values from -0.5 to 0.5
Outputs:
- pair_grad: float32 [2, 2, 256, 256, 128], P('section', None, 'row', 'col')
- grad_ln_gain: float32 [2, 128], P('section')
- grad_ln_bias: float32 [2, 128], P('section')
- grad_proj: float32 [2, 128, 512], P('section')
- grad_gate: float32 [2, 128, 128], P('section')
- grad_out_gain: float32 [2, 128], P('section')
- grad_out_bias: float32 [2, 128], P('section')
- grad_out_weight: float32 [2, 128, 128], P('section')
Inputs may be any that keep to these rules, and one draw needn't show every extreme that they name: `pad_mask`: 1 marks a real token, 0 a padding one.
All inputs are finite; a program needn't handle non-finite values.
Results may differ from a plain program's by a relative error of at most 0.0068.
Values may be sent and summed in bfloat16 or wider, within the bound.
A program may use at most 128 MiB of HBM per device.

v0:
```python
import jax
import jax.numpy as jnp
from jax import lax
from jax.sharding import PartitionSpec as P

EPSILON = 1e-05


def shifted(array, axis, by):
    length = lax.axis_size(axis)
    pairs = [(i, i + by) for i in range(length) if 0 <= i + by < length]
    return lax.ppermute(array, axis, pairs)


def layer_norm(values):
    average = jnp.mean(values, axis=-1, keepdims=True)
    centred = values - average
    variance = jnp.mean(centred * centred, axis=-1, keepdims=True)
    inverse = lax.rsqrt(variance + EPSILON)
    return (centred * inverse, inverse)


def norm_back(grad_hat, normed, inverse):
    first = jnp.mean(grad_hat, axis=-1, keepdims=True)
    second = jnp.mean(grad_hat * normed, axis=-1, keepdims=True)
    return (grad_hat - first - normed * second) * inverse


def front_part(pair_in, cell_mask, gain_in, bias_in, weight_proj, weight_gate):
    pair_hat, pair_inv = layer_norm(pair_in.astype(jnp.float32))
    normed = (pair_hat * gain_in + bias_in).astype(jnp.bfloat16)
    flat_in = normed.reshape(-1, normed.shape[-1])
    shape_lead = normed.shape[:-1]
    hidden = weight_proj.shape[1] // 4
    projected = jnp.dot(flat_in, weight_proj, preferred_element_type=jnp.float32).reshape(
        shape_lead + (4 * hidden,)
    )
    lin_a = projected[..., :hidden]
    gate_a = jax.nn.sigmoid(projected[..., hidden : 2 * hidden])
    lin_b = projected[..., 2 * hidden : 3 * hidden]
    gate_b = jax.nn.sigmoid(projected[..., 3 * hidden :])
    masked = cell_mask[..., None]
    left_proj = (gate_a * lin_a * masked).astype(jnp.bfloat16)
    right_proj = (gate_b * lin_b * masked).astype(jnp.bfloat16)
    gate_out = jax.nn.sigmoid(
        jnp.dot(flat_in, weight_gate, preferred_element_type=jnp.float32).reshape(
            shape_lead + (weight_gate.shape[1],)
        )
    )
    saved = (pair_hat, pair_inv, flat_in, lin_a, gate_a, lin_b, gate_b)
    return (left_proj, right_proj, gate_out, saved)


def out_part(pair_mix, upstream, gate_out, gain_out, bias_out, weight_out):
    mix_hat, mix_inv = layer_norm(pair_mix)
    mixed = (mix_hat * gain_out + bias_out).astype(jnp.bfloat16)
    flat_mix = mixed.reshape(-1, mixed.shape[-1])
    pair_width = weight_out.shape[1]
    outcome = jnp.dot(flat_mix, weight_out, preferred_element_type=jnp.float32).reshape(
        upstream.shape
    )
    d_outcome = (upstream * gate_out).astype(jnp.bfloat16)
    d_gate = upstream * outcome * gate_out * (1.0 - gate_out)
    flat_dout = d_outcome.reshape(-1, pair_width)
    d_mixed = lax.dot_general(
        flat_dout, weight_out, (((1,), (1,)), ((), ())), preferred_element_type=jnp.float32
    ).reshape(mix_hat.shape)
    g_weight = lax.dot_general(
        flat_mix, flat_dout, (((0,), (0,)), ((), ())), preferred_element_type=jnp.float32
    )
    hidden = mix_hat.shape[-1]
    g_gain = jnp.sum((d_mixed * mix_hat).reshape(-1, hidden), axis=0)
    g_bias = jnp.sum(d_mixed.reshape(-1, hidden), axis=0)
    d_mix = norm_back(d_mixed * gain_out, mix_hat, mix_inv).astype(jnp.bfloat16)
    return (d_mix, d_gate, (g_gain, g_bias, g_weight))


def in_part(d_left, d_right, d_gate, saved, cell_mask, upstream, gain_in, joined):
    pair_hat, pair_inv, flat_in, lin_a, gate_a, lin_b, gate_b = saved
    masked = cell_mask[..., None]
    pieces = [
        d_left * gate_a * masked,
        d_left * lin_a * masked * gate_a * (1.0 - gate_a),
        d_right * gate_b * masked,
        d_right * lin_b * masked * gate_b * (1.0 - gate_b),
        d_gate,
    ]
    d_pre = jnp.concatenate(pieces, axis=-1).astype(jnp.bfloat16)
    flat_dpre = d_pre.reshape(-1, d_pre.shape[-1])
    d_normed = lax.dot_general(
        flat_dpre, joined, (((1,), (1,)), ((), ())), preferred_element_type=jnp.float32
    ).reshape(pair_hat.shape)
    g_joined = lax.dot_general(
        flat_in, flat_dpre, (((0,), (0,)), ((), ())), preferred_element_type=jnp.float32
    )
    pair_width = pair_hat.shape[-1]
    split_at = joined.shape[1] - pair_width
    g_gain = jnp.sum((d_normed * pair_hat).reshape(-1, pair_width), axis=0)
    g_bias = jnp.sum(d_normed.reshape(-1, pair_width), axis=0)
    d_pair = norm_back(d_normed * gain_in, pair_hat, pair_inv)
    return (upstream + d_pair, (g_gain, g_bias, g_joined[:, :split_at], g_joined[:, split_at:]))


def on_device(
    pair_act,
    pair_cot,
    pad_mask,
    ln_gain,
    ln_bias,
    proj_weight,
    gate_weight,
    out_gain,
    out_bias,
    out_weight,
):
    segment_total = lax.axis_size("section")
    my_segment = lax.axis_index("section")
    micro_count = pair_cot.shape[0]
    row_count = pair_cot.shape[1]
    col_count = pair_cot.shape[2]
    pair_width = pair_cot.shape[3]
    hidden = out_weight.shape[1]
    row_start = lax.axis_index("row") * row_count
    col_start = lax.axis_index("col") * col_count
    gain_in = ln_gain[0]
    bias_in = ln_bias[0]
    weight_proj = proj_weight[0]
    weight_gate = gate_weight[0]
    gain_out = out_gain[0]
    bias_out = out_bias[0]
    weight_out = out_weight[0]
    joined = jnp.concatenate([weight_proj, weight_gate], axis=1)

    def tick_step(step, state_now):
        outgoing, pair_grads, weight_acc = state_now
        received = shifted(outgoing, "section", -1)
        slot_raw = step - (segment_total - 1 - my_segment)
        is_valid = jnp.logical_and(slot_raw >= 0, slot_raw < micro_count)
        slot_index = jnp.clip(slot_raw, 0, micro_count - 1)
        upstream = jnp.where(my_segment == segment_total - 1, pair_cot[slot_index], received)
        pair_in = pair_act[0, slot_index]
        token_mask = pad_mask[slot_index].astype(jnp.float32)
        mask_rows = lax.dynamic_slice_in_dim(token_mask, row_start, row_count)
        mask_cols = lax.dynamic_slice_in_dim(token_mask, col_start, col_count)
        cell_mask = mask_rows[:, None] * mask_cols[None, :]
        left_proj, right_proj, gate_out, saved = front_part(
            pair_in, cell_mask, gain_in, bias_in, weight_proj, weight_gate
        )
        right_all = lax.all_gather(right_proj, "row", axis=0, tiled=True)
        partial_value = jnp.einsum(
            "ikh,jkh->ijh", left_proj, right_all, preferred_element_type=jnp.float32
        )
        pair_mix = lax.psum_scatter(partial_value, "col", scatter_dimension=1, tiled=True)
        d_mix, d_gate, out_grads = out_part(
            pair_mix, upstream, gate_out, gain_out, bias_out, weight_out
        )
        d_mix_all = lax.all_gather(d_mix, "col", axis=1, tiled=True)
        d_left = jnp.einsum(
            "ijh,jkh->ikh", d_mix_all, right_all, preferred_element_type=jnp.float32
        )
        right_terms = jnp.einsum(
            "ijh,ikh->jkh", d_mix_all, left_proj, preferred_element_type=jnp.float32
        )
        d_right = lax.psum_scatter(right_terms, "row", scatter_dimension=0, tiled=True)
        new_grad, in_grads = in_part(
            d_left, d_right, d_gate, saved, cell_mask, upstream, gain_in, joined
        )
        kept_grad = jnp.where(is_valid, new_grad, pair_grads[slot_index])
        pair_grads = pair_grads.at[slot_index].set(kept_grad)
        keep_mask = is_valid.astype(jnp.float32)
        grads = in_grads + out_grads
        weight_acc = tuple((total + keep_mask * term for total, term in zip(weight_acc, grads)))
        return (new_grad, pair_grads, weight_acc)

    start_acc = (
        jnp.zeros((pair_width,), jnp.float32),
        jnp.zeros((pair_width,), jnp.float32),
        jnp.zeros((pair_width, 4 * hidden), jnp.float32),
        jnp.zeros((pair_width, pair_width), jnp.float32),
        jnp.zeros((hidden,), jnp.float32),
        jnp.zeros((hidden,), jnp.float32),
        jnp.zeros((hidden, pair_width), jnp.float32),
    )
    start_state = (
        jnp.zeros((row_count, col_count, pair_width), jnp.float32),
        jnp.zeros((micro_count, row_count, col_count, pair_width), jnp.float32),
        start_acc,
    )
    final_state = lax.fori_loop(0, segment_total + micro_count - 1, tick_step, start_state)
    pair_grads = final_state[1]
    summed = lax.psum(final_state[2], ("row", "col"))
    return (
        pair_grads[None],
        summed[0][None],
        summed[1][None],
        summed[2][None],
        summed[3][None],
        summed[4][None],
        summed[5][None],
        summed[6][None],
    )


def solution(mesh):
    placed = (
        P("section", None, "row", "col", None),
        P(None, "row", "col", None),
        P(),
        P("section", None),
        P("section", None),
        P("section", None, None),
        P("section", None, None),
        P("section", None),
        P("section", None),
        P("section", None, None),
    )
    return jax.shard_map(
        on_device,
        mesh=mesh,
        in_specs=placed,
        out_specs=(
            P("section", None, "row", "col", None),
            P("section", None),
            P("section", None),
            P("section", None, None),
            P("section", None, None),
            P("section", None),
            P("section", None),
            P("section", None, None),
        ),
        check_vma=False,
    )
```

profile of v0, /device:TPU:0, one launch (start us, length us, event | category | flops | bytes accessed | tf_op | source)
XLA Modules:
  0.0 969.7 jit_solution(5008346442208482857)
XLA Ops:
  10.9 768.4 %while.33 = (s32[]{:T(128)}, f32[64,16,128]{2,1,0:T(8,128)}, f32[2,64,16,128]{3,2,1,0:T(8,128)}, f32[128]{0:T(128)}, f32[128]{0:T(128)}, /*index=5*/f32[128,512]...) while((s32[]{:T(128)}, f32[64,16,128]{2,1,0:T(8,128)}, ...), condition=%wide.region_16.17_spmd.clone, body=%wide.region_0.16_spmd.clone.sunk | while | flops 821858560 | bytes 184999792 | solution.py:189
  16.6 25.2 %all-gather.3.cloned.1.call-done = bf16[256,16,128]{2,1,0:T(8,128)(2,1)} async-done(((bf16[64,16,128]{2,1,0:T(8,128)(2,1)}), bf16[256,16,128]{2,1,0:T(8,128)(2,1)}) %all-gather.3.cloned.1.call-update) | async-done | bytes 1048592 | tf_op jit(solution)/shard_map/while/body/eval_jaxpr/all_gather | solution.py:149
  49.6 8.8 copy.160
  67.9 76.3 %reduce-scatter.3.cloned.1.call-done = f32[64,16,128]{2,0,1:T(8,128)} async-done(((f32[64,256,128]{2,0,1:T(8,128)}), f32[64,16,128]{2,0,1:T(8,128)}) %reduce-scatter.3.cloned.1.call-update) | async-done | bytes 524304 | tf_op jit(solution)/shard_map/while/body/eval_jaxpr/reduce_scatter | solution.py:153
  150.9 51.0 %all-gather.5.cloned.1.call-done = bf16[64,256,128]{2,0,1:T(8,128)(2,1)} async-done(((bf16[64,16,128]{2,0,1:T(8,128)(2,1)}), bf16[64,256,128]{2,0,1:T(8,128)(2,1)}) %all-gather.5.cloned.1.call-update) | async-done | bytes 4194320 | tf_op jit(solution)/shard_map/while/body/eval_jaxpr/all_gather | solution.py:157
  201.9 12.9 %copy.162 = bf16[64,256,128]{0,1,2:T(8,128)(2,1)} copy(bf16[64,256,128]{2,0,1:T(8,128)(2,1)} %all-gather.5.cloned.1.call-done) | data formatting | bytes 8388608 | tf_op jit(solution)/shard_map/while/body/eval_jaxpr/all_gather | solution.py:157
  214.8 7.2 fusion.103
  231.7 6.0 fusion.102
  242.5 12.2 %reduce-scatter.5.cloned.1.call-done = f32[64,16,128]{2,1,0:T(8,128)} async-done(((f32[256,16,128]{2,1,0:T(8,128)}), f32[64,16,128]{2,1,0:T(8,128)}) %reduce-scatter.5.cloned.1.call-update) | async-done | bytes 524304 | tf_op jit(solution)/shard_map/while/body/eval_jaxpr/reduce_scatter | solution.py:164
  274.6 22.5 %all-gather.3.cloned.1.call-done = bf16[256,16,128]{2,1,0:T(8,128)(2,1)} async-done(((bf16[64,16,128]{2,1,0:T(8,128)(2,1)}), bf16[256,16,128]{2,1,0:T(8,128)(2,1)}) %all-gather.3.cloned.1.call-update) | async-done | bytes 1048592 | tf_op jit(solution)/shard_map/while/body/eval_jaxpr/all_gather | solution.py:149
  304.8 8.8 copy.160
  324.3 75.2 %reduce-scatter.3.cloned.1.call-done = f32[64,16,128]{2,0,1:T(8,128)} async-done(((f32[64,256,128]{2,0,1:T(8,128)}), f32[64,16,128]{2,0,1:T(8,128)}) %reduce-scatter.3.cloned.1.call-update) | async-done | bytes 524304 | tf_op jit(solution)/shard_map/while/body/eval_jaxpr/reduce_scatter | solution.py:153
  406.1 51.0 %all-gather.5.cloned.1.call-done = bf16[64,256,128]{2,0,1:T(8,128)(2,1)} async-done(((bf16[64,16,128]{2,0,1:T(8,128)(2,1)}), bf16[64,256,128]{2,0,1:T(8,128)(2,1)}) %all-gather.5.cloned.1.call-update) | async-done | bytes 4194320 | tf_op jit(solution)/shard_map/while/body/eval_jaxpr/all_gather | solution.py:157
  457.1 12.9 %copy.162 = bf16[64,256,128]{0,1,2:T(8,128)(2,1)} copy(bf16[64,256,128]{2,0,1:T(8,128)(2,1)} %all-gather.5.cloned.1.call-done) | data formatting | bytes 8388608 | tf_op jit(solution)/shard_map/while/body/eval_jaxpr/all_gather | solution.py:157
  470.0 7.2 fusion.103
  499.0 11.0 %reduce-scatter.5.cloned.1.call-done = f32[64,16,128]{2,1,0:T(8,128)} async-done(((f32[256,16,128]{2,1,0:T(8,128)}), f32[64,16,128]{2,1,0:T(8,128)}) %reduce-scatter.5.cloned.1.call-update) | async-done | bytes 524304 | tf_op jit(solution)/shard_map/while/body/eval_jaxpr/reduce_scatter | solution.py:164
  529.8 22.5 %all-gather.3.cloned.1.call-done = bf16[256,16,128]{2,1,0:T(8,128)(2,1)} async-done(((bf16[64,16,128]{2,1,0:T(8,128)(2,1)}), bf16[256,16,128]{2,1,0:T(8,128)(2,1)}) %all-gather.3.cloned.1.call-update) | async-done | bytes 1048592 | tf_op jit(solution)/shard_map/while/body/eval_jaxpr/all_gather | solution.py:149
  560.0 8.8 copy.160
  579.4 75.2 %reduce-scatter.3.cloned.1.call-done = f32[64,16,128]{2,0,1:T(8,128)} async-done(((f32[64,256,128]{2,0,1:T(8,128)}), f32[64,16,128]{2,0,1:T(8,128)}) %reduce-scatter.3.cloned.1.call-update) | async-done | bytes 524304 | tf_op jit(solution)/shard_map/while/body/eval_jaxpr/reduce_scatter | solution.py:153
  661.2 51.0 %all-gather.5.cloned.1.call-done = bf16[64,256,128]{2,0,1:T(8,128)(2,1)} async-done(((bf16[64,16,128]{2,0,1:T(8,128)(2,1)}), bf16[64,256,128]{2,0,1:T(8,128)(2,1)}) %all-gather.5.cloned.1.call-update) | async-done | bytes 4194320 | tf_op jit(solution)/shard_map/while/body/eval_jaxpr/all_gather | solution.py:157
  712.2 12.9 %copy.162 = bf16[64,256,128]{0,1,2:T(8,128)(2,1)} copy(bf16[64,256,128]{2,0,1:T(8,128)(2,1)} %all-gather.5.cloned.1.call-done) | data formatting | bytes 8388608 | tf_op jit(solution)/shard_map/while/body/eval_jaxpr/all_gather | solution.py:157
  725.1 7.2 fusion.103
  754.1 11.0 %reduce-scatter.5.cloned.1.call-done = f32[64,16,128]{2,1,0:T(8,128)} async-done(((f32[256,16,128]{2,1,0:T(8,128)}), f32[64,16,128]{2,1,0:T(8,128)}) %reduce-scatter.5.cloned.1.call-update) | async-done | bytes 524304 | tf_op jit(solution)/shard_map/while/body/eval_jaxpr/reduce_scatter | solution.py:164
  779.8 177.8 %all-reduce = (f32[1,128]{1,0:T(1,128)}, f32[1,128]{1,0:T(1,128)}, f32[1,128]{1,0:T(1,128)}, f32[1,128]{1,0:T(1,128)}) all-reduce(f32[1,128]{1,0:T(1,128)} %bitcast.228, f32[1,128]{1,0:T(1,128)} %bitcast.229, f32[1,128]{1,0:T(1,128)} %bitcast.226, f32[1,128]{1,0:T(1,128)} %bitcast.227), channel_id=1, replica_groups=mesh['section'=2,'row'=4,'col'=16] {'row','col'}, use_global_device_ids=true, to_apply=%region_17.18 | all-reduce | flops 512 | bytes 4096 | tf_op jit(solution)/shard_map/psum | solution.py:191
  (388 shorter events, 198.2 us)
Async XLA Ops:
  10.9 30.9 %all-gather.3.cloned.1.call-start = ((), (), s32[]{:S(2)}) async-start(), calls=%async_computation.3 | async-start | bytes 1310720 | tf_op jit(solution)/shard_map/while/body/eval_jaxpr/all_gather | solution.py:149
  15.2 129.0 %reduce-scatter.3.cloned.1.call-start = ((), (), s32[]{:S(2)}) async-start(), calls=%async_computation.4 | async-start | bytes 8912896 | tf_op jit(solution)/shard_map/while/body/eval_jaxpr/reduce_scatter | solution.py:153
  58.4 143.5 %all-gather.5.cloned.1.call-start = ((), (), s32[]{:S(2)}) async-start(), calls=%async_computation.5 | async-start | bytes 4456448 | tf_op jit(solution)/shard_map/while/body/eval_jaxpr/all_gather | solution.py:157
  58.5 3.8 collective-permute-start
  65.0 82.1 %copy-start.15 = (bf16[64,16,128]{2,1,0:T(8,128)(2,1)}, bf16[64,16,128]{2,1,0:T(8,128)(2,1)S(1)}, u32[]{:S(2)}) copy-start(bf16[64,16,128]{2,1,0:T(8,128)(2,1)S(1)} %get-tuple-element.937) | copy-start | bytes 786436 | tf_op jit(solution)/shard_map/while
  145.5 3.3 copy-start
  145.5 3.3 copy-start.1
  150.9 103.9 %reduce-scatter.5.cloned.1.call-start = ((), (), s32[]{:S(2)}) async-start(), calls=%async_computation.6 | async-start | bytes 2621440 | tf_op jit(solution)/shard_map/while/body/eval_jaxpr/reduce_scatter | solution.py:164
  225.3 3.4 copy-start.24
  268.9 28.1 %all-gather.3.cloned.1.call-start = ((), (), s32[]{:S(2)}) async-start(), calls=%async_computation.3 | async-start | bytes 1310720 | tf_op jit(solution)/shard_map/while/body/eval_jaxpr/all_gather | solution.py:149
  273.2 126.2 %reduce-scatter.3.cloned.1.call-start = ((), (), s32[]{:S(2)}) async-start(), calls=%async_computation.4 | async-start | bytes 8912896 | tf_op jit(solution)/shard_map/while/body/eval_jaxpr/reduce_scatter | solution.py:153
  313.7 143.4 %all-gather.5.cloned.1.call-start = ((), (), s32[]{:S(2)}) async-start(), calls=%async_computation.5 | async-start | bytes 4456448 | tf_op jit(solution)/shard_map/while/body/eval_jaxpr/all_gather | solution.py:157
  314.8 3.8 collective-permute-start
  321.3 81.0 %copy-start.15 = (bf16[64,16,128]{2,1,0:T(8,128)(2,1)}, bf16[64,16,128]{2,1,0:T(8,128)(2,1)S(1)}, u32[]{:S(2)}) copy-start(bf16[64,16,128]{2,1,0:T(8,128)(2,1)S(1)} %get-tuple-element.937) | copy-start | bytes 786436 | tf_op jit(solution)/shard_map/while
  406.0 103.9 %reduce-scatter.5.cloned.1.call-start = ((), (), s32[]{:S(2)}) async-start(), calls=%async_computation.6 | async-start | bytes 2621440 | tf_op jit(solution)/shard_map/while/body/eval_jaxpr/reduce_scatter | solution.py:164
  480.5 3.4 copy-start.24
  524.1 28.1 %all-gather.3.cloned.1.call-start = ((), (), s32[]{:S(2)}) async-start(), calls=%async_computation.3 | async-start | bytes 1310720 | tf_op jit(solution)/shard_map/while/body/eval_jaxpr/all_gather | solution.py:149
  528.4 126.2 %reduce-scatter.3.cloned.1.call-start = ((), (), s32[]{:S(2)}) async-start(), calls=%async_computation.4 | async-start | bytes 8912896 | tf_op jit(solution)/shard_map/while/body/eval_jaxpr/reduce_scatter | solution.py:153
  568.9 143.3 %all-gather.5.cloned.1.call-start = ((), (), s32[]{:S(2)}) async-start(), calls=%async_computation.5 | async-start | bytes 4456448 | tf_op jit(solution)/shard_map/while/body/eval_jaxpr/all_gather | solution.py:157
  570.0 3.8 collective-permute-start
  576.4 81.0 %copy-start.15 = (bf16[64,16,128]{2,1,0:T(8,128)(2,1)}, bf16[64,16,128]{2,1,0:T(8,128)(2,1)S(1)}, u32[]{:S(2)}) copy-start(bf16[64,16,128]{2,1,0:T(8,128)(2,1)S(1)} %get-tuple-element.937) | copy-start | bytes 786436 | tf_op jit(solution)/shard_map/while
  661.2 103.9 %reduce-scatter.5.cloned.1.call-start = ((), (), s32[]{:S(2)}) async-start(), calls=%async_computation.6 | async-start | bytes 2621440 | tf_op jit(solution)/shard_map/while/body/eval_jaxpr/reduce_scatter | solution.py:164
  735.6 3.4 copy-start.24
  779.2 178.4 %all-reduce.4.cloned.1.call-start = ((), (), s32[]{:S(2)}) async-start(), calls=%async_computation.2 | async-start | bytes 786432 | tf_op jit(solution)/shard_map/psum | solution.py:191
  (75 other events, 159.1 us)
Sparse Core Ops, SparseCore 0:
  15.4 26.3 all-gather.2
  58.6 85.6 reduce-scatter.2
  151.0 50.8 all-gather.4
  225.5 29.2 reduce-scatter.4
  273.3 23.6 all-gather.2
  313.8 85.5 reduce-scatter.2
  406.2 50.8 all-gather.4
  480.6 29.2 reduce-scatter.4
  528.5 23.6 all-gather.2
  569.0 85.5 reduce-scatter.2
  661.3 50.8 all-gather.4
  735.7 29.2 reduce-scatter.4
Sparse Core Ops, SparseCore 1:
  785.2 127.1 all-reduce.3
where the time goes:
time: 973 us; the launch traced here: 970 us
  waiting for transfers between devices  492 us (51%)
  blocking collectives  178 us (18%)
  local copies, waits for them, and re-layouts  127 us (13%)
  matrix products  94.3 us (10%)
  other arithmetic  57.4 us (6%)
  between operations  15.6 us (2%)
    reduce_scatter x3, waiting for transfers between devices, tick_step(): lax.psum_scatter(partial_value, 'col', scatter_dimension=1, tiled=True)  227 us
    psum x1, blocking collectives, on_device(): summed = lax.psum(final_state[2], ('row', 'col'))  178 us
    all_gather x3, waiting for transfers between devices, tick_step(): d_mix_all = lax.all_gather(d_mix, 'col', axis=1, tiled=True)  153 us
    all_gather x3, waiting for transfers between devices, tick_step(): right_all = lax.all_gather(right_proj, 'row', axis=0, tiled=True)  70.1 us
    all_gather x3, local copies, waits for them, and re-layouts, tick_step(): d_mix_all = lax.all_gather(d_mix, 'col', axis=1, tiled=True)  38.8 us
    reduce_scatter x3, waiting for transfers between devices, tick_step(): lax.psum_scatter(right_terms, 'row', scatter_dimension=0, tiled=True)  34.1 us
    transpose x3, local copies, waits for them, and re-layouts, tick_step(): jnp.einsum('ikh,jkh->ijh', left_proj, right_all, preferred_element_type=j...  26.5 us
    dot_general x3, matrix products, tick_step(): jnp.einsum('ijh,ikh->jkh', d_mix_all, left_proj, preferred_element_type=j...  21.5 us
  transfers between devices with their start and end apart: 16, of which 15 were waited for; matrix products, arithmetic and copies ran while one was open for 8% of the time, Pallas kernels for 0%

commit v1 on v0

v1 whole, which is shorter than its diff:
```python
import jax
import jax.numpy as jnp
from jax import lax
from jax.experimental import pallas as pl
from jax.experimental.pallas import tpu as pltpu
from jax.sharding import PartitionSpec as P

EPSILON = 1e-05
MESH = pl.DeviceIdType.MESH
F32 = jnp.float32
BF16 = jnp.bfloat16
ROWS = 4
COLS = 16
PEERS = ROWS * COLS
N = 1024
WIDE = 256

X_COPY, W_COPY, O_COPY, V_COPY, PG_COPY = range(5)
LR, MIX, DMIX, DLR, RS = range(5)


def sigmoid(v):
    return 0.5 * jnp.tanh(0.5 * v) + 0.5


def mean0(v):
    return jnp.mean(v, axis=0, keepdims=True)


def dot(a, b, ca=1, cb=0):
    return lax.dot_general(a, b, (((ca,), (cb,)), ((), ())), preferred_element_type=F32)


def kernel(
    act_ref, cot_ref, mask_v, mask_sm, lng_ref, lnb_ref, proj_ref, gatew_ref, og_ref, ob_ref, outw_ref,
    pg_ref, glng_ref, glnb_ref, gproj_ref, ggate_ref, gog_ref, gob_ref, gow_ref,
    xs, w_s, wo_s, vec_s, xf, wt_s, wot_s, gain_s, mask_s,
    hat_s, inv_s, nrm_s, la_s, ga_s, lb_s, gb_s, go_s,
    mhat_s, minv_s, mn_s, oc_s, up_s, dout_s, dpre_s, acc_s,
    scr_a, scr_b, lt_s, rt_s, dt_s,
    send_lr, recv_lr, send_m, recv_m, send_d, recv_d, send_g, recv_g,
    pgb, gs, recv_b, send_c, recv_c, recv_o,
    psend, precv, ssem, rsem, csem, dsem,
):
    m, r, c = lax.axis_index("section"), lax.axis_index("row"), lax.axis_index("col")
    me = r * COLS + c
    other = 1 - m
    partner = (other, r, c)

    barrier = pltpu.get_barrier_semaphore()

    def greet(k, carry):
        d = lax.rem(me + k, PEERS)
        pl.semaphore_signal(barrier, inc=1, device_id=(m, d // COLS, lax.rem(d, COLS)), device_id_type=MESH)
        return carry

    def greet_row(k, carry):
        pl.semaphore_signal(barrier, inc=1, device_id=(other, r, k), device_id_type=MESH)
        return carry

    lax.fori_loop(1, PEERS, greet, 0)
    lax.fori_loop(0, COLS, greet_row, 0)

    low = lax.broadcasted_iota(jnp.int32, (128, 128), 1) < 64
    low1 = lax.broadcasted_iota(jnp.int32, (8, 128), 1) < 64

    def exchange(src, dst, phase, sec):
        def send(k, carry):
            d = lax.rem(me + k, PEERS)
            pltpu.make_async_remote_copy(
                src.at[sec, d], dst.at[sec, me], ssem.at[phase, sec], rsem.at[phase, sec],
                device_id=(m, d // COLS, lax.rem(d, COLS)), device_id_type=MESH,
            ).start()
            return carry

        lax.fori_loop(1, PEERS, send, 0)
        dst[sec, me] = src[sec, me]

    def arrived(dst, phase, sec):
        part = dst.at[sec, pl.ds(0, PEERS - 1)]
        pltpu.make_async_copy(part, part, rsem.at[phase, sec]).wait()

    def sent(src, phase, sec):
        part = src.at[sec, pl.ds(0, PEERS - 1)]
        pltpu.make_async_copy(part, part, ssem.at[phase, sec]).wait()

    def lanes(b):
        return pl.ds(pl.multiple_of(b * WIDE, WIDE), WIDE)

    def cells_to_lanes(src, b):
        out = []
        for u in range(2):
            t = 2 * b + u
            rows = jnp.concatenate([src[pl.ds(t, 64, stride=16), :], src[pl.ds(t + 8, 64, stride=16), :]], axis=0)
            out.append(rows.T)
        return jnp.concatenate(out, axis=1)

    def lanes_to_cells(value, dst, b):
        for u in range(2):
            t = 2 * b + u
            rows = value[:, 128 * u:128 * u + 128].T
            dst[pl.ds(t, 64, stride=16), :] = rows[:64]
            dst[pl.ds(t + 8, 64, stride=16), :] = rows[64:]

    def spread(value, dst, b):
        for u in range(2):
            dst[pl.ds(2 * b + u, 128, stride=8), :] = value[:, 128 * u:128 * u + 128]

    def gathered(src, b):
        return jnp.concatenate([src[pl.ds(2 * b + u, 128, stride=8), :] for u in range(2)], axis=1)

    def wide(g):
        return jnp.concatenate([g, g], axis=1)

    whole = jnp.where(m == 0, mask_v[0:1, :], mask_v[1:2, :]).astype(F32)
    half = jnp.broadcast_to(jnp.where(r >= 2, whole[:, 128:], whole[:, :128]), (8, 128))
    turned = pltpu.roll(half, 64, 1)
    is_even = lax.rem(r, 2) == 0
    mask_i = jnp.where(low1, jnp.where(is_even, half, turned), jnp.where(is_even, turned, half))
    for t in range(8):
        first = mask_sm[m, c * 16 + t].astype(F32)
        second = mask_sm[m, c * 16 + 8 + t].astype(F32)
        mask_s[:, 128 * t:128 * t + 128] = mask_i * jnp.where(low1, first, second)

    def prepare(sec):
        wt_s[sec] = w_s[sec].astype(F32).T.astype(BF16)
        wot_s[sec] = wo_s[sec].astype(F32).T.astype(BF16)
        for v in range(4):
            gain_s[sec, v] = jnp.broadcast_to(vec_s[sec, v:v + 1, :], (128, 128)).T

    def front(sec):
        prepare(sec)
        xf[...] = xs[sec].astype(F32)

        def block(b, carry):
            at = lanes(b)
            x = cells_to_lanes(xf, b)
            centred = x - mean0(x)
            inv = lax.rsqrt(mean0(centred * centred) + EPSILON)
            hat = centred * inv
            nrm = (hat * wide(gain_s[sec, 0]) + wide(gain_s[sec, 1])).astype(BF16)
            hat_s[sec, :, at] = hat
            inv_s[sec, :, at] = jnp.broadcast_to(inv, (8, WIDE))
            nrm_s[sec, :, at] = nrm
            mask = mask_s[0:1, at]
            lin = dot(wt_s[sec, 0:128], nrm)
            gate = sigmoid(dot(wt_s[sec, 128:256], nrm))
            la_s[sec, :, at] = lin
            ga_s[sec, :, at] = gate
            spread(gate * lin * mask, scr_a, b)
            lin = dot(wt_s[sec, 256:384], nrm)
            gate = sigmoid(dot(wt_s[sec, 384:512], nrm))
            lb_s[sec, :, at] = lin
            gb_s[sec, :, at] = gate
            spread(gate * lin * mask, scr_b, b)
            go_s[sec, :, at] = sigmoid(dot(wt_s[sec, 512:640], nrm))
            return carry

        lax.fori_loop(0, 4, block, 0)
        send_lr[sec, :, 0:16, :] = scr_a[...].reshape(PEERS, 16, 128).astype(BF16)
        send_lr[sec, :, 16:32, :] = scr_b[...].reshape(PEERS, 16, 128).astype(BF16)

    def assemble(src, sec, at, dst, first):
        for q in range(2):
            even = src[sec, 32 * q:32 * q + 16, at:at + 16, :].astype(F32)
            odd = src[sec, 32 * q + 16:32 * q + 32, at:at + 16, :].astype(F32)
            for ch in range(2):
                a = even[:, 8 * ch:8 * ch + 8, :].reshape(128, 128)
                b = odd[:, 8 * ch:8 * ch + 8, :].reshape(128, 128)
                k0 = jnp.where(low, a, pltpu.roll(b, 64, 1)).reshape(16, 1, 8, 128)
                k1 = jnp.where(low, pltpu.roll(a, 64, 1), b).reshape(16, 1, 8, 128)
                full = jnp.concatenate([k0, k1], axis=1).reshape(256, 128)
                dst[first + ch, :, 128 * q:128 * q + 128] = full.astype(BF16)

    def take_apart(pair, dst, sec, at):
        for q in range(2):
            evens, odds = [], []
            for y in pair:
                y4 = y[:, 128 * q:128 * q + 128].reshape(16, 2, 8, 128)
                y0 = y4[:, 0].reshape(128, 128)
                y1 = y4[:, 1].reshape(128, 128)
                evens.append(jnp.where(low, y0, pltpu.roll(y1, 64, 1)).reshape(16, 8, 128))
                odds.append(jnp.where(low, pltpu.roll(y0, 64, 1), y1).reshape(16, 8, 128))
            dst[sec, 32 * q:32 * q + 16, at:at + 16, :] = jnp.concatenate(evens, axis=1).astype(BF16)
            dst[sec, 32 * q + 16:32 * q + 32, at:at + 16, :] = jnp.concatenate(odds, axis=1).astype(BF16)

    def mix(sec):
        arrived(recv_lr, LR, sec)
        assemble(recv_lr, sec, 0, lt_s, 2 * sec)
        assemble(recv_lr, sec, 16, rt_s, 2 * sec)
        pair = [dot(rt_s[2 * sec + ch], lt_s[2 * sec + ch], 0, 0) for ch in range(2)]
        take_apart(pair, send_m, sec, 0)
        exchange(send_m, recv_m, MIX, sec)

    def out_forward(sec):
        arrived(recv_m, MIX, sec)
        scr_a[...] = recv_m[sec].astype(F32).reshape(N, 128)

        def block(b, carry):
            at = lanes(b)
            x = gathered(scr_a, b)
            centred = x - mean0(x)
            inv = lax.rsqrt(mean0(centred * centred) + EPSILON)
            hat = centred * inv
            mn = (hat * wide(gain_s[sec, 2]) + wide(gain_s[sec, 3])).astype(BF16)
            mhat_s[sec, :, at] = hat
            minv_s[sec, :, at] = jnp.broadcast_to(inv, (8, WIDE))
            mn_s[sec, :, at] = mn
            gate = go_s[sec, :, at]
            oc_s[sec, :, at] = dot(wot_s[sec], mn) * gate * (1.0 - gate)
            return carry

        lax.fori_loop(0, 4, block, 0)

    def out_backward(sec):
        acc_s[2] = jnp.zeros((128, WIDE), F32)
        acc_s[3] = jnp.zeros((128, WIDE), F32)

        def block(b, carry):
            at = lanes(b)
            up = up_s[sec, :, at]
            dout = (up * go_s[sec, :, at]).astype(BF16)
            dout_s[:, at] = dout
            dpre_s[512:640, at] = (up * oc_s[sec, :, at]).astype(BF16)
            dn = dot(wo_s[sec], dout)
            hat = mhat_s[sec, :, at]
            acc_s[2] += dn * hat
            acc_s[3] += dn
            e = dn * wide(gain_s[sec, 2])
            d = (e - mean0(e) - hat * mean0(e * hat)) * minv_s[sec, 0:1, at]
            spread(d, scr_b, b)
            return carry

        lax.fori_loop(0, 4, block, 0)
        send_d[sec] = scr_b[...].reshape(PEERS, 16, 128).astype(BF16)
        exchange(send_d, recv_d, DMIX, sec)

    def products_back(sec):
        arrived(recv_d, DMIX, sec)
        assemble(recv_d, sec, 0, dt_s, 0)
        pair = [dot(rt_s[2 * sec + ch], dt_s[ch]) for ch in range(2)]
        take_apart(pair, send_g, sec, 0)
        pair = [dot(lt_s[2 * sec + ch], dt_s[ch], 1, 1) for ch in range(2)]
        take_apart(pair, send_g, sec, 16)
        exchange(send_g, recv_g, DLR, sec)

    def in_part(sec):
        acc_s[0] = jnp.zeros((128, WIDE), F32)
        acc_s[1] = jnp.zeros((128, WIDE), F32)
        arrived(recv_g, DLR, sec)
        scr_a[...] = recv_g[sec, :, 0:16, :].astype(F32).reshape(N, 128)
        scr_b[...] = recv_g[sec, :, 16:32, :].astype(F32).reshape(N, 128)

        def block(b, carry):
            at = lanes(b)
            mask = mask_s[0:1, at]
            gate = ga_s[sec, :, at]
            dg = gathered(scr_a, b) * gate * mask
            dpre_s[0:128, at] = dg.astype(BF16)
            dpre_s[128:256, at] = (dg * la_s[sec, :, at] * (1.0 - gate)).astype(BF16)
            gate = gb_s[sec, :, at]
            dg = gathered(scr_b, b) * gate * mask
            dpre_s[256:384, at] = dg.astype(BF16)
            dpre_s[384:512, at] = (dg * lb_s[sec, :, at] * (1.0 - gate)).astype(BF16)
            din = dot(w_s[sec], dpre_s[:, at])
            hat = hat_s[sec, :, at]
            acc_s[0] += din * hat
            acc_s[1] += din
            f = din * wide(gain_s[sec, 0])
            up = up_s[sec, :, at] + (f - mean0(f) - hat * mean0(f * hat)) * inv_s[sec, 0:1, at]
            if sec > 0:
                up_s[sec - 1, :, at] = up
            lanes_to_cells(up, pgb.at[sec], b)
            return carry

        lax.fori_loop(0, 4, block, 0)

    def weight_grads(sec):
        for o in range(5):
            g = dot(nrm_s[sec], dpre_s[128 * o:128 * o + 128, :], 1, 1)
            gs[sec, :, 8 * o:8 * o + 8, :] = g.reshape(COLS, 8, 128)
        for v in range(4):
            total = (acc_s[v, :, 0:128] + acc_s[v, :, 128:256]).T
            gs[sec, 0, 48 + v:49 + v, :] = jnp.sum(total, axis=0, keepdims=True)

    def out_weight_grads(sec):
        gs[sec, :, 40:48, :] = dot(mn_s[sec], dout_s[...], 1, 1).reshape(COLS, 8, 128)

    def scatter_grads(sec):
        def send(k, carry):
            d = lax.rem(c + k, COLS)

            @pl.when(jnp.logical_or(m != sec, k > 0))
            def _():
                pltpu.make_async_remote_copy(
                    gs.at[sec, d], recv_b.at[m * COLS + c], ssem.at[RS, sec], rsem.at[RS, 0],
                    device_id=(sec, r, d), device_id_type=MESH,
                ).start()

            return carry

        lax.fori_loop(0, COLS, send, 0)

        @pl.when(m == sec)
        def _():
            recv_b[sec * COLS + c] = gs[sec, c]

    xs[m] = act_ref[m]
    w_s[m, :, 0:512] = proj_ref[...]
    w_s[m, :, 512:640] = gatew_ref[...]
    wo_s[m] = outw_ref[...]
    vec_s[m, 0:1] = lng_ref[...]
    vec_s[m, 1:2] = lnb_ref[...]
    vec_s[m, 2:3] = og_ref[...]
    vec_s[m, 3:4] = ob_ref[...]
    vec_s[m, 4:8] = jnp.zeros((4, 128), F32)
    for sec in range(2):
        gs[sec, :, 48:56, :] = jnp.zeros((COLS, 8, 128), F32)

    front(m)
    pl.semaphore_wait(barrier, PEERS - 1 + COLS)
    swaps = [
        pltpu.make_async_remote_copy(
            src, dst, psend.at[n], precv.at[n], device_id=partner, device_id_type=MESH
        )
        for n, (src, dst) in enumerate(
            [(act_ref.at[other], xs.at[m]), (w_s.at[m], w_s.at[m]), (wo_s.at[m], wo_s.at[m]), (vec_s.at[m], vec_s.at[m])]
        )
    ]
    for swap in swaps:
        swap.start()
    exchange(send_lr, recv_lr, LR, m)

    def turn(b, carry):
        up_s[1, :, lanes(b)] = cells_to_lanes(cot_ref.at[m], b)
        return carry

    lax.fori_loop(0, 4, turn, 0)
    for swap in swaps:
        swap.wait_recv()
    front(other)
    exchange(send_lr, recv_lr, LR, other)

    mix(m)
    mix(other)
    out_forward(1)
    out_backward(1)
    out_forward(0)
    out_weight_grads(1)
    products_back(1)
    in_part(1)
    weight_grads(1)
    out_backward(0)
    scatter_grads(1)
    out_weight_grads(0)
    products_back(0)
    in_part(0)
    handed = pltpu.make_async_remote_copy(
        pgb.at[other], pg_ref.at[m], psend.at[PG_COPY], precv.at[PG_COPY], device_id=partner, device_id_type=MESH
    )
    handed.start()
    weight_grads(0)
    scatter_grads(0)
    pg_ref[m] = pgb[m]

    part = recv_b.at[pl.ds(0, 2 * COLS - 1)]
    pltpu.make_async_copy(part, part, rsem.at[RS, 0]).wait()
    total = jnp.sum(recv_b[...], axis=0)
    send_c[...] = total
    recv_c[r] = total
    for k in range(1, ROWS):
        pltpu.make_async_remote_copy(
            send_c, recv_c.at[r], csem.at[0], csem.at[1],
            device_id=(m, lax.rem(r + k, ROWS), c), device_id_type=MESH,
        ).start()
    part = recv_c.at[pl.ds(0, ROWS - 1)]
    pltpu.make_async_copy(part, part, csem.at[1]).wait()
    recv_o[c] = jnp.sum(recv_c[...], axis=0)

    def give(k, carry):
        pltpu.make_async_remote_copy(
            recv_o.at[c], recv_o.at[c], dsem.at[0], dsem.at[1],
            device_id=(m, r, lax.rem(c + k, COLS)), device_id_type=MESH,
        ).start()
        return carry

    lax.fori_loop(1, COLS, give, 0)
    for src, phase in ((send_lr, LR), (send_m, MIX), (send_d, DMIX), (send_g, DLR)):
        for sec in range(2):
            sent(src, phase, sec)
    for sec in range(2):
        part = gs.at[sec, pl.ds(0, COLS - 1)]
        pltpu.make_async_copy(part, part, ssem.at[RS, sec]).wait()

        @pl.when(m != sec)
        def _():
            part = gs.at[sec, 0]
            pltpu.make_async_copy(part, part, ssem.at[RS, sec]).wait()

    part = recv_c.at[pl.ds(0, ROWS - 1)]
    pltpu.make_async_copy(part, part, csem.at[0]).wait()
    for swap in swaps:
        swap.wait_send()
    part = recv_o.at[pl.ds(0, COLS - 1)]
    pltpu.make_async_copy(part, part, dsem.at[0]).wait()
    pltpu.make_async_copy(part, part, dsem.at[1]).wait()
    for o in range(4):
        gproj_ref[:, 128 * o:128 * o + 128] = recv_o[:, 8 * o:8 * o + 8, :].reshape(128, 128)
    ggate_ref[...] = recv_o[:, 32:40, :].reshape(128, 128)
    gow_ref[...] = recv_o[:, 40:48, :].reshape(128, 128)
    glng_ref[...] = recv_o[0, 48:49, :]
    glnb_ref[...] = recv_o[0, 49:50, :]
    gog_ref[...] = recv_o[0, 50:51, :]
    gob_ref[...] = recv_o[0, 51:52, :]
    handed.wait()


def on_device(act, cot, mask, lng, lnb, proj, gatew, og, ob, outw):
    vmem = pl.BlockSpec(memory_space=pltpu.VMEM)
    smem = pl.BlockSpec(memory_space=pltpu.SMEM)

    def v(shape, dtype=F32):
        return pltpu.VMEM(shape, dtype)

    sds = jax.ShapeDtypeStruct
    results = pl.pallas_call(
        kernel,
        out_shape=(
            sds((2, N, 128), F32), sds((1, 128), F32), sds((1, 128), F32), sds((128, 512), F32),
            sds((128, 128), F32), sds((1, 128), F32), sds((1, 128), F32), sds((128, 128), F32),
        ),
        in_specs=[vmem, vmem, vmem, smem] + [vmem] * 7,
        out_specs=(vmem,) * 8,
        scratch_shapes=[
            v((2, N, 128), BF16), v((2, 128, 640), BF16), v((2, 128, 128), BF16), v((2, 8, 128)), v((N, 128)),
            v((2, 640, 128), BF16), v((2, 128, 128), BF16), v((2, 4, 128, 128)), v((8, N)),
            v((2, 128, N)), v((2, 8, N)), v((2, 128, N), BF16),
            v((2, 128, N)), v((2, 128, N)), v((2, 128, N)), v((2, 128, N)), v((2, 128, N)),
            v((2, 128, N)), v((2, 8, N)), v((2, 128, N), BF16), v((2, 128, N)), v((2, 128, N)),
            v((128, N), BF16), v((640, N), BF16), v((4, 128, WIDE)),
            v((N, 128)), v((N, 128)), v((4, 256, 256), BF16), v((4, 256, 256), BF16), v((2, 256, 256), BF16),
            v((2, PEERS, 32, 128), BF16), v((2, PEERS, 32, 128), BF16),
            v((2, PEERS, 16, 128), BF16), v((2, PEERS, 16, 128), BF16),
            v((2, PEERS, 16, 128), BF16), v((2, PEERS, 16, 128), BF16),
            v((2, PEERS, 32, 128), BF16), v((2, PEERS, 32, 128), BF16),
            v((2, N, 128)), v((2, COLS, 56, 128)), v((2 * COLS, 56, 128)),
            v((56, 128)), v((ROWS, 56, 128)), v((COLS, 56, 128)),
            pltpu.SemaphoreType.DMA((5,)), pltpu.SemaphoreType.DMA((5,)),
            pltpu.SemaphoreType.DMA((5, 2)), pltpu.SemaphoreType.DMA((5, 2)),
            pltpu.SemaphoreType.DMA((2,)), pltpu.SemaphoreType.DMA((2,)),
        ],
        compiler_params=pltpu.CompilerParams(
            collective_id=1, has_side_effects=True, vmem_limit_bytes=56 * 2**20
        ),
    )(
        act.reshape(2, N, 128), cot.reshape(2, N, 128), mask, mask, lng, lnb, proj[0], gatew[0], og, ob, outw[0]
    )
    pg, glng, glnb, gproj, ggate, gog, gob, gow = results
    return (
        pg.reshape(1, 2, 64, 16, 128), glng, glnb, gproj[None], ggate[None], gog, gob, gow[None],
    )


def solution(mesh):
    vector, matrix = P("section", None), P("section", None, None)
    grid = P("section", None, "row", "col", None)
    return jax.shard_map(
        on_device,
        mesh=mesh,
        in_specs=(grid, P(None, "row", "col", None), P(), vector, vector, matrix, matrix, vector, vector, matrix),
        out_specs=(grid, vector, vector, matrix, matrix, vector, vector, matrix),
        check_vma=False,
    )
```

time: 973 us -> 105 us (0.11)
  waiting for transfers between devices: 492 us -> 0 us
  blocking collectives: 178 us -> 0 us
  local copies, waits for them, and re-layouts: 127 us -> 6.8 us
  Pallas kernels: 0 us -> 97.5 us
  matrix products: 94.3 us -> 0 us
  other arithmetic: 57.4 us -> 0 us
  between operations: 15.6 us -> 0.67 us
    reduce_scatter x6 -> x0, waiting for transfers between devices: 261 us -> none  [the longest x3 227 us: tick_step(): lax.psum_scatter(partial_value, 'col', scatter_dimension=1, tiled=True)]
    all_gather x6 -> x0, waiting for transfers between devices: 223 us -> none  [the longest x3 153 us: tick_step(): d_mix_all = lax.all_gather(d_mix, 'col', axis=1, tiled=True)]
    psum x1 -> x0, blocking collectives: 178 us -> none  [on_device(): summed = lax.psum(final_state[2], ('row', 'col'))]
    pallas_call x0 -> x1, Pallas kernels: none -> 97.5 us  [on_device(): pl.pallas_call(kernel, out_shape=(sds((2, N, 128), F32), sds((1, 128), F3...]
    dot_general x30 -> x0, matrix products: 94.3 us -> none  [the longest x3 21.5 us: tick_step(): jnp.einsum('ijh,ikh->jkh', d_mix_all, left_proj, preferred_element_type=j...]
    all_gather x6 -> x0, local copies, waits for them, and re-layouts: 45.4 us -> none  [the longest x3 38.8 us: tick_step(): d_mix_all = lax.all_gather(d_mix, 'col', axis=1, tiled=True)]
    transpose x3 -> x0, local copies, waits for them, and re-layouts: 26.5 us -> none  [tick_step(): jnp.einsum('ikh,jkh->ijh', left_proj, right_all, preferred_element_type=j...]
    while x168 -> x0, local copies, waits for them, and re-layouts: 15.4 us -> none
  transfers between devices with their start and end apart: 16 -> 0, of which waited for: 15 -> 0; matrix products, arithmetic and copies ran while one was open for 8% -> 0% of each run, Pallas kernels for 0% -> 0%
where the time goes in v1:
time: 105 us
  Pallas kernels  97.5 us (93%)
  local copies, waits for them, and re-layouts  6.8 us (6%)
    pallas_call x1, Pallas kernels, on_device(): pl.pallas_call(kernel, out_shape=(sds((2, N, 128), F32), sds((1, 128), F3...  97.5 us
    unnamed x22, local copies, waits for them, and re-layouts  6.8 us

profile of v1, /device:TPU:0, one launch (start us, length us, event | category | flops | bytes accessed | tf_op | source)
XLA Modules:
  0.0 105.0 jit_solution(11288157201361768241)
XLA Ops:
  0.6 97.5 %shard_map.161 = (f32[2,1024,128]{2,1,0:T(8,128)}, f32[1,128]{1,0:T(1,128)}, f32[1,128]{1,0:T(1,128)}, f32[128,512]{1,0:T(8,128)}, f32[128,128]{1,0:T(8,128)}, /...) custom-call(bf16[2,1024,128]{2,1,0:T(8,128)(2,1)} %bitcast.11, f32[2,1024,128]{2,1,0:T(8,128)} %bitcast.9, ...), custom_call_target="tpu_custom_call" | custom-call | tf_op jit(solution)/shard_map/pallas_call | solution.py:426
  98.2 0.0 copy-start.6
  98.2 0.0 copy-start
  98.2 2.3 %copy.26 = f32[1,2,64,16,128]{4,3,2,1,0:T(8,128)} copy(f32[1,2,64,16,128]{4,3,2,1,0:T(8,128)} %bitcast.10) | data formatting | bytes 2097152
  100.5 0.0 copy-done.6
  100.5 0.0 copy-start.5
  100.5 0.5 copy.27
  101.0 0.2 copy-done.5
  101.2 0.5 copy.28
  101.7 0.0 copy-done
  101.7 0.0 copy-start.2
  101.7 0.7 copy.29
  102.4 0.2 copy-done.2
  102.6 0.0 copy-start.4
  102.6 0.0 copy-start.1
  102.6 0.6 copy.30
  103.2 0.0 copy-done.4
  103.2 0.0 copy-start.3
  103.2 0.5 copy.31
  103.7 0.2 copy-done.3
  103.9 0.5 copy.32
  104.4 0.0 copy-done.1
  104.4 0.6 copy.33
Async XLA Ops:
  98.2 2.3 %copy-start.6 = (f32[1,128]{1,0:T(1,128)S(1)}, f32[1,128]{1,0:T(1,128)}, u32[]{:S(2)}) copy-start(f32[1,128]{1,0:T(1,128)} %get-tuple-element.33) | copy-start | bytes 1540
  98.2 3.5 %copy-start = (f32[128,512]{1,0:T(8,128)S(1)}, f32[128,512]{1,0:T(8,128)}, u32[]{:S(2)}) copy-start(f32[128,512]{1,0:T(8,128)} %get-tuple-element.19) | copy-start | bytes 786436
  100.5 0.7 copy-start.5
  101.7 0.9 copy-start.2
  102.6 0.6 copy-start.4
  102.6 1.8 %copy-start.1 = (f32[128,128]{1,0:T(8,128)S(1)}, f32[128,128]{1,0:T(8,128)}, u32[]{:S(2)}) copy-start(f32[128,128]{1,0:T(8,128)} %get-tuple-element.23) | copy-start | bytes 196612
  103.2 0.7 copy-start.3

commit v2 on v1

v2 whole, which is shorter than its diff:
```python
import jax
import jax.numpy as jnp
from jax import lax
from jax.experimental import pallas as pl
from jax.experimental.pallas import tpu as pltpu
from jax.sharding import PartitionSpec as P

EPSILON = 1e-05
MESH = pl.DeviceIdType.MESH
F32 = jnp.float32
BF16 = jnp.bfloat16
ROWS = 4
COLS = 16
PEERS = ROWS * COLS
N = 1024
WIDE = 256

X_COPY, W_COPY, O_COPY, V_COPY, PG_COPY = range(5)
LR, MIX, DMIX, DLR, RS = range(5)
OWNERS = 49


def sigmoid(v):
    return 0.5 * jnp.tanh(0.5 * v) + 0.5


def mean0(v):
    return jnp.mean(v, axis=0, keepdims=True)


def dot(a, b, ca=1, cb=0):
    return lax.dot_general(a, b, (((ca,), (cb,)), ((), ())), preferred_element_type=F32)


def kernel(
    act_ref, cot_ref, mask_v, mask_sm, lng_ref, lnb_ref, proj_ref, gatew_ref, og_ref, ob_ref, outw_ref,
    pg_ref, recv_o,
    xs, w_s, wo_s, vec_s, xf, wt_s, wot_s, gain_s, mask_s,
    hat_s, inv_s, nrm_s, la_s, ga_s, lb_s, gb_s, go_s,
    mhat_s, minv_s, mn_s, oc_s, up_s, dout_s, dpre_s, acc_s,
    scr_a, scr_b, lt_s, rt_s, dt_s,
    send_lr, recv_lr, send_m, recv_m, send_d, recv_d, send_g, recv_g,
    pgb, gs, recv_b,
    psend, precv, ssem, rsem, dsem,
):
    m, r, c = lax.axis_index("section"), lax.axis_index("row"), lax.axis_index("col")
    me = r * COLS + c
    other = 1 - m
    partner = (other, r, c)

    z, y = c // 4, lax.rem(c, 4)

    def step4(v):
        return jnp.where(v == 0, 2, jnp.where(v == 3, 0, 2 * v - 1))

    def peer(k):
        to_r = lax.rem(r + step4(lax.rem(k, 4)), 4)
        to_c = lax.rem(z + step4(k // 16), 4) * 4 + lax.rem(y + step4(lax.rem(k // 4, 4)), 4)
        return to_r, to_c, to_r * COLS + to_c

    barrier = pltpu.get_barrier_semaphore()

    def greet(k, carry):
        to_r, to_c, _ = peer(k)
        pl.semaphore_signal(barrier, inc=1, device_id=(other, to_r, to_c), device_id_type=MESH)

        @pl.when(k < PEERS - 1)
        def _():
            pl.semaphore_signal(barrier, inc=1, device_id=(m, to_r, to_c), device_id_type=MESH)

        return carry

    lax.fori_loop(0, PEERS, greet, 0)

    low = lax.broadcasted_iota(jnp.int32, (128, 128), 1) < 64
    low1 = lax.broadcasted_iota(jnp.int32, (8, 128), 1) < 64

    def exchange(src, dst, phase, sec):
        def send(k, carry):
            to_r, to_c, d = peer(k)
            pltpu.make_async_remote_copy(
                src.at[sec, d], dst.at[sec, me], ssem.at[phase, sec], rsem.at[phase, sec],
                device_id=(m, to_r, to_c), device_id_type=MESH,
            ).start()
            return carry

        lax.fori_loop(0, PEERS - 1, send, 0)
        dst[sec, me] = src[sec, me]

    def exchange_lr():
        def send(k, carry):
            to_r, to_c, d = peer(k)
            for dest in (m, other):
                def start(dest=dest):
                    pltpu.make_async_remote_copy(
                        send_lr.at[dest, d], recv_lr.at[m, me], ssem.at[LR, dest], rsem.at[LR, m],
                        device_id=(dest, to_r, to_c), device_id_type=MESH,
                    ).start()

                if dest is m:
                    pl.when(k < PEERS - 1)(start)
                else:
                    start()
            return carry

        lax.fori_loop(0, PEERS, send, 0)
        recv_lr[m, me] = send_lr[m, me]

    def arrived_lr(sec):
        @pl.when(m == sec)
        def _():
            arrived(recv_lr, LR, sec)

        @pl.when(m != sec)
        def _():
            part = recv_lr.at[sec]
            pltpu.make_async_copy(part, part, rsem.at[LR, sec]).wait()


    def arrived(dst, phase, sec):
        part = dst.at[sec, pl.ds(0, PEERS - 1)]
        pltpu.make_async_copy(part, part, rsem.at[phase, sec]).wait()

    def sent(src, phase, sec):
        part = src.at[sec, pl.ds(0, PEERS - 1)]
        pltpu.make_async_copy(part, part, ssem.at[phase, sec]).wait()

    def lanes(b):
        return pl.ds(pl.multiple_of(b * WIDE, WIDE), WIDE)

    def cells_to_lanes(src, b):
        out = []
        for u in range(2):
            t = 2 * b + u
            rows = jnp.concatenate([src[pl.ds(t, 64, stride=16), :], src[pl.ds(t + 8, 64, stride=16), :]], axis=0)
            out.append(rows.T)
        return jnp.concatenate(out, axis=1)

    def lanes_to_cells(value, dst, b):
        for u in range(2):
            t = 2 * b + u
            rows = value[:, 128 * u:128 * u + 128].T
            dst[pl.ds(t, 64, stride=16), :] = rows[:64]
            dst[pl.ds(t + 8, 64, stride=16), :] = rows[64:]

    def spread(value, dst, b):
        for u in range(2):
            dst[pl.ds(2 * b + u, 128, stride=8), :] = value[:, 128 * u:128 * u + 128]

    def gathered(src, b):
        return jnp.concatenate([src[pl.ds(2 * b + u, 128, stride=8), :] for u in range(2)], axis=1)

    def wide(g):
        return jnp.concatenate([g, g], axis=1)

    is_even = lax.rem(r, 2) == 0
    for n in range(2):
        whole = mask_v[n:n + 1, :].astype(F32)
        half = jnp.broadcast_to(jnp.where(r >= 2, whole[:, 128:], whole[:, :128]), (8, 128))
        turned = pltpu.roll(half, 64, 1)
        mask_i = jnp.where(low1, jnp.where(is_even, half, turned), jnp.where(is_even, turned, half))
        for t in range(8):
            first = mask_sm[n, c * 16 + t].astype(F32)
            second = mask_sm[n, c * 16 + 8 + t].astype(F32)
            mask_s[n, :, 128 * t:128 * t + 128] = mask_i * jnp.where(low1, first, second)

    def prepare(sec):
        wt_s[sec] = w_s[sec].astype(F32).T.astype(BF16)
        wot_s[sec] = wo_s[sec].astype(F32).T.astype(BF16)
        for v in range(4):
            gain_s[sec, v] = jnp.broadcast_to(vec_s[sec, v:v + 1, :], (128, 128)).T

    def front(sec, source, save, target):
        xf[...] = source[...].astype(F32)

        def block(b, carry):
            at = lanes(b)
            x = cells_to_lanes(xf, b)
            centred = x - mean0(x)
            inv = lax.rsqrt(mean0(centred * centred) + EPSILON)
            hat = centred * inv
            nrm = (hat * wide(gain_s[sec, 0]) + wide(gain_s[sec, 1])).astype(BF16)
            lin_a = dot(wt_s[sec, 0:128], nrm)
            gate_a = sigmoid(dot(wt_s[sec, 128:256], nrm))
            lin_b = dot(wt_s[sec, 256:384], nrm)
            gate_b = sigmoid(dot(wt_s[sec, 384:512], nrm))
            if target is not None:
                mask = mask_s[target, 0:1, at]
                spread(gate_a * lin_a * mask, scr_a, b)
                spread(gate_b * lin_b * mask, scr_b, b)
            if save:
                hat_s[sec, :, at] = hat
                inv_s[sec, :, at] = jnp.broadcast_to(inv, (8, WIDE))
                nrm_s[sec, :, at] = nrm
                la_s[sec, :, at] = lin_a
                ga_s[sec, :, at] = gate_a
                lb_s[sec, :, at] = lin_b
                gb_s[sec, :, at] = gate_b
                go_s[sec, :, at] = sigmoid(dot(wt_s[sec, 512:640], nrm))
            return carry

        lax.fori_loop(0, 4, block, 0)
        if target is not None:
            send_lr[target, :, 0:16, :] = scr_a[...].reshape(PEERS, 16, 128).astype(BF16)
            send_lr[target, :, 16:32, :] = scr_b[...].reshape(PEERS, 16, 128).astype(BF16)

    def assemble(src, sec, at, dst, first):
        for q in range(2):
            even = src[sec, 32 * q:32 * q + 16, at:at + 16, :].astype(F32)
            odd = src[sec, 32 * q + 16:32 * q + 32, at:at + 16, :].astype(F32)
            for ch in range(2):
                a = even[:, 8 * ch:8 * ch + 8, :].reshape(128, 128)
                b = odd[:, 8 * ch:8 * ch + 8, :].reshape(128, 128)
                k0 = jnp.where(low, a, pltpu.roll(b, 64, 1)).reshape(16, 1, 8, 128)
                k1 = jnp.where(low, pltpu.roll(a, 64, 1), b).reshape(16, 1, 8, 128)
                full = jnp.concatenate([k0, k1], axis=1).reshape(256, 128)
                dst[first + ch, :, 128 * q:128 * q + 128] = full.astype(BF16)

    def take_apart(pair, dst, sec, at):
        for q in range(2):
            evens, odds = [], []
            for y in pair:
                y4 = y[:, 128 * q:128 * q + 128].reshape(16, 2, 8, 128)
                y0 = y4[:, 0].reshape(128, 128)
                y1 = y4[:, 1].reshape(128, 128)
                evens.append(jnp.where(low, y0, pltpu.roll(y1, 64, 1)).reshape(16, 8, 128))
                odds.append(jnp.where(low, pltpu.roll(y0, 64, 1), y1).reshape(16, 8, 128))
            dst[sec, 32 * q:32 * q + 16, at:at + 16, :] = jnp.concatenate(evens, axis=1).astype(BF16)
            dst[sec, 32 * q + 16:32 * q + 32, at:at + 16, :] = jnp.concatenate(odds, axis=1).astype(BF16)

    def mix(sec):
        arrived_lr(sec)
        assemble(recv_lr, sec, 0, lt_s, 2 * sec)
        assemble(recv_lr, sec, 16, rt_s, 2 * sec)
        pair = [dot(rt_s[2 * sec + ch], lt_s[2 * sec + ch], 0, 0) for ch in range(2)]
        take_apart(pair, send_m, sec, 0)
        exchange(send_m, recv_m, MIX, sec)

    def out_forward(sec):
        arrived(recv_m, MIX, sec)
        scr_a[...] = recv_m[sec].astype(F32).reshape(N, 128)

        def block(b, carry):
            at = lanes(b)
            x = gathered(scr_a, b)
            centred = x - mean0(x)
            inv = lax.rsqrt(mean0(centred * centred) + EPSILON)
            hat = centred * inv
            mn = (hat * wide(gain_s[sec, 2]) + wide(gain_s[sec, 3])).astype(BF16)
            mhat_s[sec, :, at] = hat
            minv_s[sec, :, at] = jnp.broadcast_to(inv, (8, WIDE))
            mn_s[sec, :, at] = mn
            gate = go_s[sec, :, at]
            oc_s[sec, :, at] = dot(wot_s[sec], mn) * gate * (1.0 - gate)
            return carry

        lax.fori_loop(0, 4, block, 0)

    def out_backward(sec):
        acc_s[sec, 2] = jnp.zeros((128, WIDE), F32)
        acc_s[sec, 3] = jnp.zeros((128, WIDE), F32)

        def block(b, carry):
            at = lanes(b)
            up = up_s[sec, :, at]
            dout = (up * go_s[sec, :, at]).astype(BF16)
            dout_s[sec, :, at] = dout
            dpre_s[sec, 512:640, at] = (up * oc_s[sec, :, at]).astype(BF16)
            dn = dot(wo_s[sec], dout)
            hat = mhat_s[sec, :, at]
            acc_s[sec, 2] += dn * hat
            acc_s[sec, 3] += dn
            e = dn * wide(gain_s[sec, 2])
            d = (e - mean0(e) - hat * mean0(e * hat)) * minv_s[sec, 0:1, at]
            spread(d, scr_b, b)
            return carry

        lax.fori_loop(0, 4, block, 0)
        send_d[sec] = scr_b[...].reshape(PEERS, 16, 128).astype(BF16)
        exchange(send_d, recv_d, DMIX, sec)

    def products_back(sec):
        arrived(recv_d, DMIX, sec)
        assemble(recv_d, sec, 0, dt_s, 0)
        pair = [dot(rt_s[2 * sec + ch], dt_s[ch]) for ch in range(2)]
        take_apart(pair, send_g, sec, 0)
        pair = [dot(lt_s[2 * sec + ch], dt_s[ch], 1, 1) for ch in range(2)]
        take_apart(pair, send_g, sec, 16)
        exchange(send_g, recv_g, DLR, sec)

    def in_part(sec):
        acc_s[sec, 0] = jnp.zeros((128, WIDE), F32)
        acc_s[sec, 1] = jnp.zeros((128, WIDE), F32)
        arrived(recv_g, DLR, sec)
        scr_a[...] = recv_g[sec, :, 0:16, :].astype(F32).reshape(N, 128)
        scr_b[...] = recv_g[sec, :, 16:32, :].astype(F32).reshape(N, 128)

        def block(b, carry):
            at = lanes(b)
            mask = mask_s[m, 0:1, at]
            gate = ga_s[sec, :, at]
            dg = gathered(scr_a, b) * gate * mask
            dpre_s[sec, 0:128, at] = dg.astype(BF16)
            dpre_s[sec, 128:256, at] = (dg * la_s[sec, :, at] * (1.0 - gate)).astype(BF16)
            gate = gb_s[sec, :, at]
            dg = gathered(scr_b, b) * gate * mask
            dpre_s[sec, 256:384, at] = dg.astype(BF16)
            dpre_s[sec, 384:512, at] = (dg * lb_s[sec, :, at] * (1.0 - gate)).astype(BF16)
            din = dot(w_s[sec], dpre_s[sec, :, at])
            hat = hat_s[sec, :, at]
            acc_s[sec, 0] += din * hat
            acc_s[sec, 1] += din
            f = din * wide(gain_s[sec, 0])
            up = up_s[sec, :, at] + (f - mean0(f) - hat * mean0(f * hat)) * inv_s[sec, 0:1, at]
            up_s[sec - 1 if sec > 0 else 2, :, at] = up
            return carry

        lax.fori_loop(0, 4, block, 0)

    def back_to_cells(sec):
        def block(b, carry):
            lanes_to_cells(up_s[sec - 1 if sec > 0 else 2, :, lanes(b)], pgb.at[sec], b)
            return carry

        lax.fori_loop(0, 4, block, 0)

    def early_grads(sec):
        g = dot(nrm_s[sec], dpre_s[sec, 512:640, :], 1, 1)
        gs[sec, 32:40] = g.reshape(8, 16, 128).astype(BF16)
        g = dot(mn_s[sec], dout_s[sec], 1, 1)
        gs[sec, 40:48] = g.reshape(8, 16, 128).astype(BF16)
        scatter_grads(sec, True)

    def late_grads(sec):
        for o in range(4):
            g = dot(nrm_s[sec], dpre_s[sec, 128 * o:128 * o + 128, :], 1, 1)
            gs[sec, 8 * o:8 * o + 8] = g.reshape(8, 16, 128).astype(BF16)
        rows = []
        for v in range(4):
            total = (acc_s[sec, v, :, 0:128] + acc_s[sec, v, :, 128:256]).T
            rows.append(jnp.sum(total, axis=0, keepdims=True))
        rows = jnp.concatenate(rows + [jnp.zeros((4, 128), F32)], axis=0)
        high = rows.astype(BF16).astype(F32)
        gs[sec, 48] = jnp.concatenate([high, rows - high], axis=0).astype(BF16)
        scatter_grads(sec, False)

    def scatter_grads(sec, early):
        def send(k, carry):
            to_r, to_c, d = peer(k)
            in_early = jnp.logical_and(d >= 32, d < 48)
            wanted = in_early if early else jnp.logical_and(d < OWNERS, jnp.logical_not(in_early))
            away = jnp.logical_or(m != sec, k < PEERS - 1)

            @pl.when(jnp.logical_and(wanted, away))
            def _():
                pltpu.make_async_remote_copy(
                    gs.at[sec, d], recv_b.at[m * PEERS + me], ssem.at[RS, sec], rsem.at[RS, 0],
                    device_id=(sec, to_r, to_c), device_id_type=MESH,
                ).start()

            @pl.when(jnp.logical_and(wanted, jnp.logical_not(away)))
            def _():
                recv_b[m * PEERS + me] = gs[sec, d]

            return carry

        lax.fori_loop(0, PEERS, send, 0)

    def gather_grads():
        @pl.when(me < OWNERS)
        def _():
            part = recv_b.at[pl.ds(0, 2 * PEERS - 1)]
            pltpu.make_async_copy(part, part, rsem.at[RS, 0]).wait()
            recv_o[me] = jnp.sum(recv_b[...].astype(F32), axis=0)

            def give(k, carry):
                to_r, to_c, _ = peer(k)
                pltpu.make_async_remote_copy(
                    recv_o.at[me], recv_o.at[me], dsem.at[0], dsem.at[1],
                    device_id=(m, to_r, to_c), device_id_type=MESH,
                ).start()
                return carry

            lax.fori_loop(0, PEERS - 1, give, 0)

    xs[m] = act_ref[m]
    w_s[m, :, 0:512] = proj_ref[...]
    w_s[m, :, 512:640] = gatew_ref[...]
    wo_s[m] = outw_ref[...]
    vec_s[m, 0:1] = lng_ref[...]
    vec_s[m, 1:2] = lnb_ref[...]
    vec_s[m, 2:3] = og_ref[...]
    vec_s[m, 3:4] = ob_ref[...]
    vec_s[m, 4:8] = jnp.zeros((4, 128), F32)

    prepare(m)
    front(m, act_ref.at[m], True, m)
    front(m, act_ref.at[other], False, other)
    pl.semaphore_wait(barrier, 2 * PEERS - 1)

    @pl.when(m == 1)
    def _():
        exchange_lr()

    swaps = [
        pltpu.make_async_remote_copy(
            src, dst, psend.at[n], precv.at[n], device_id=partner, device_id_type=MESH
        )
        for n, (src, dst) in enumerate(
            [(act_ref.at[other], xs.at[m]), (w_s.at[m], w_s.at[m]), (wo_s.at[m], wo_s.at[m]), (vec_s.at[m], vec_s.at[m])]
        )
    ]
    for swap in swaps:
        swap.start()

    def turn(b, carry):
        up_s[1, :, lanes(b)] = cells_to_lanes(cot_ref.at[m], b)
        return carry

    lax.fori_loop(0, 4, turn, 0)
    for swap in swaps:
        swap.wait_recv()
    prepare(other)
    front(other, xs.at[other], True, None)

    mix(1)

    @pl.when(m == 0)
    def _():
        exchange_lr()

    out_forward(1)
    out_backward(1)
    mix(0)
    early_grads(1)
    products_back(1)
    out_forward(0)
    in_part(1)
    out_backward(0)
    late_grads(1)
    back_to_cells(1)
    handed = pltpu.make_async_remote_copy(
        pgb.at[other], pg_ref.at[m], psend.at[PG_COPY], precv.at[PG_COPY], device_id=partner, device_id_type=MESH
    )

    @pl.when(m == 0)
    def _():
        handed.start()

    @pl.when(m == 1)
    def _():
        pg_ref[1] = pgb[1]

    products_back(0)
    early_grads(0)

    @pl.when(m == 1)
    def _():
        gather_grads()

    in_part(0)
    late_grads(0)
    back_to_cells(0)

    @pl.when(m == 1)
    def _():
        handed.start()

    @pl.when(m == 0)
    def _():
        pg_ref[0] = pgb[0]
        gather_grads()

    for src, phase in ((send_m, MIX), (send_d, DMIX), (send_g, DLR)):
        for sec in range(2):
            sent(src, phase, sec)
    sent(send_lr, LR, m)
    part = send_lr.at[other]
    pltpu.make_async_copy(part, part, ssem.at[LR, other]).wait()
    for sec in range(2):
        own_rows = jnp.logical_and(m == sec, me < OWNERS)
        for count, which in ((OWNERS - 1, own_rows), (OWNERS, jnp.logical_not(own_rows))):

            @pl.when(which)
            def _(count=count, sec=sec):
                part = gs.at[sec, pl.ds(0, count)]
                pltpu.make_async_copy(part, part, ssem.at[RS, sec]).wait()

    for swap in swaps:
        swap.wait_send()
    handed.wait()

    @pl.when(me >= OWNERS)
    def _():
        part = recv_o.at[pl.ds(0, OWNERS)]
        pltpu.make_async_copy(part, part, dsem.at[1]).wait()

    @pl.when(me < OWNERS)
    def _():
        part = recv_o.at[pl.ds(0, OWNERS - 1)]
        pltpu.make_async_copy(part, part, dsem.at[1]).wait()
        part = recv_o.at[pl.ds(0, PEERS - 1)]
        pltpu.make_async_copy(part, part, dsem.at[0]).wait()


def write_out(pg_in, o_ref, pg_ref, glng_ref, glnb_ref, gproj_ref, ggate_ref, gog_ref, gob_ref, gow_ref, held, sem_in, sem_out):
    parts = [pl.ds(n * 256, 256) for n in range(8)]
    come = [pltpu.make_async_copy(pg_in.at[p], held.at[p], sem_in.at[n]) for n, p in enumerate(parts)]
    go = [pltpu.make_async_copy(held.at[p], pg_ref.at[p], sem_out.at[n]) for n, p in enumerate(parts)]
    for copy in come:
        copy.start()
    for o in range(4):
        gproj_ref[:, 128 * o:128 * o + 128] = o_ref[8 * o:8 * o + 8].reshape(128, 128)
    ggate_ref[...] = o_ref[32:40].reshape(128, 128)
    gow_ref[...] = o_ref[40:48].reshape(128, 128)
    for v, ref in enumerate((glng_ref, glnb_ref, gog_ref, gob_ref)):
        ref[...] = o_ref[48, v:v + 1, :] + o_ref[48, 8 + v:9 + v, :]
    for copy_in, copy_out in zip(come, go):
        copy_in.wait()
        copy_out.start()
    for copy in go:
        copy.wait()


def on_device(act, cot, mask, lng, lnb, proj, gatew, og, ob, outw):
    vmem = pl.BlockSpec(memory_space=pltpu.VMEM)
    smem = pl.BlockSpec(memory_space=pltpu.SMEM)

    def v(shape, dtype=F32):
        return pltpu.VMEM(shape, dtype)

    sds = jax.ShapeDtypeStruct
    pg, rows = pl.pallas_call(
        kernel,
        out_shape=(sds((2, N, 128), F32), sds((PEERS, 16, 128), F32)),
        in_specs=[vmem, vmem, vmem, smem] + [vmem] * 7,
        out_specs=(vmem,) * 2,
        scratch_shapes=[
            v((2, N, 128), BF16), v((2, 128, 640), BF16), v((2, 128, 128), BF16), v((2, 8, 128)), v((N, 128)),
            v((2, 640, 128), BF16), v((2, 128, 128), BF16), v((2, 4, 128, 128)), v((2, 8, N)),
            v((2, 128, N)), v((2, 8, N)), v((2, 128, N), BF16),
            v((2, 128, N)), v((2, 128, N)), v((2, 128, N)), v((2, 128, N)), v((2, 128, N)),
            v((2, 128, N)), v((2, 8, N)), v((2, 128, N), BF16), v((2, 128, N)), v((3, 128, N)),
            v((2, 128, N), BF16), v((2, 640, N), BF16), v((2, 4, 128, WIDE)),
            v((N, 128)), v((N, 128)), v((4, 256, 256), BF16), v((4, 256, 256), BF16), v((2, 256, 256), BF16),
            v((2, PEERS, 32, 128), BF16), v((2, PEERS, 32, 128), BF16),
            v((2, PEERS, 16, 128), BF16), v((2, PEERS, 16, 128), BF16),
            v((2, PEERS, 16, 128), BF16), v((2, PEERS, 16, 128), BF16),
            v((2, PEERS, 32, 128), BF16), v((2, PEERS, 32, 128), BF16),
            v((2, N, 128)), v((2, OWNERS, 16, 128), BF16), v((2 * PEERS, 16, 128), BF16),
            pltpu.SemaphoreType.DMA((5,)), pltpu.SemaphoreType.DMA((5,)),
            pltpu.SemaphoreType.DMA((5, 2)), pltpu.SemaphoreType.DMA((5, 2)),
            pltpu.SemaphoreType.DMA((2,)),
        ],
        compiler_params=pltpu.CompilerParams(
            collective_id=1, has_side_effects=True, vmem_limit_bytes=56 * 2**20
        ),
    )(
        act.reshape(2, N, 128), cot.reshape(2, N, 128), mask, mask, lng, lnb, proj[0], gatew[0], og, ob, outw[0]
    )
    anywhere = pl.BlockSpec(memory_space=pl.ANY)
    pg, glng, glnb, gproj, ggate, gog, gob, gow = pl.pallas_call(
        write_out,
        out_shape=(
            sds((2 * N, 128), F32), sds((1, 128), F32), sds((1, 128), F32), sds((128, 512), F32),
            sds((128, 128), F32), sds((1, 128), F32), sds((1, 128), F32), sds((128, 128), F32),
        ),
        in_specs=[anywhere, vmem],
        out_specs=(anywhere,) + (vmem,) * 7,
        scratch_shapes=[v((2 * N, 128)), pltpu.SemaphoreType.DMA((8,)), pltpu.SemaphoreType.DMA((8,))],
    )(pg.reshape(2 * N, 128), rows)
    return (
        pg.reshape(1, 2, 64, 16, 128), glng, glnb, gproj[None], ggate[None], gog, gob, gow[None],
    )


def solution(mesh):
    vector, matrix = P("section", None), P("section", None, None)
    grid = P("section", None, "row", "col", None)
    return jax.shard_map(
        on_device,
        mesh=mesh,
        in_specs=(grid, P(None, "row", "col", None), P(), vector, vector, matrix, matrix, vector, vector, matrix),
        out_specs=(grid, vector, vector, matrix, matrix, vector, vector, matrix),
        check_vma=False,
    )
```

time: 105 us -> 93.7 us (0.89)
  local copies, waits for them, and re-layouts: 6.8 us -> 0 us
  Pallas kernels: 97.5 us -> 92.7 us
    unnamed x22 -> x0, local copies, waits for them, and re-layouts: 6.8 us -> none
    pallas_call x1 -> x2, Pallas kernels: 97.5 us -> 92.7 us  [the longest x1 88.8 us: on_device(): pl.pallas_call(kernel, out_shape=(sds((2, N, 128), F32), sds((PEERS, 16,...]
where the time goes in v2:
time: 93.7 us; the launch traced here: 93.4 us
  Pallas kernels  92.7 us (99%)
    pallas_call x1, Pallas kernels, on_device(): pl.pallas_call(kernel, out_shape=(sds((2, N, 128), F32), sds((PEERS, 16,...  88.8 us
    pallas_call x1, Pallas kernels, on_device(): pl.pallas_call(write_out, out_shape=(sds((2 * N, 128), F32), sds((1, 128)...  3.88 us

profile of v2, /device:TPU:0, one launch (start us, length us, event | category | flops | bytes accessed | tf_op | source)
XLA Modules:
  0.0 93.4 jit_solution(17071586894561862753)
XLA Ops:
  0.6 88.8 %shard_map.161 = (f32[2,1024,128]{2,1,0:T(8,128)}, f32[64,16,128]{2,1,0:T(8,128)}) custom-call(bf16[2,1024,128]{2,1,0:T(8,128)(2,1)} %bitcast.12, f32[2,1024,128]{2,1,0:T(8,128)} %bitcast.11, s32[2,256]{1,0:T(2,128)} %mask_sm.1, s32[2,256]{1,0:T(2,128)} %mask_sm.1, f32[1,128]{1,0:T(1,128)} %lng_ref.1, f32[1,128]{1,0:T(1,128)} %lnb_ref.1, ...), custom_call_target="tpu_custom_call" | custom-call | tf_op jit(solution)/shard_map/pallas_call | solution.py:533
  89.5 3.9 %shard_map.162 = (f32[2048,128]{1,0:T(8,128)}, f32[1,128]{1,0:T(1,128)}, f32[1,128]{1,0:T(1,128)}, f32[128,512]{1,0:T(8,128)}, f32[128,128]{1,0:T(8,128)}, /*ind...) custom-call(f32[2048,128]{1,0:T(8,128)} %bitcast.10, f32[64,16,128]{2,1,0:T(8,128)} %get-tuple-element.19.o_ref), custom_call_target="tpu_custom_call" | custom-call | tf_op jit(solution)/shard_map/pallas_call | solution.py:562

commit v3 on v2

--- a/solution.py
+++ b/solution.py
@@ -33,15 +33,15 @@
 
 
 def kernel(
-    act_ref, cot_ref, mask_v, mask_sm, lng_ref, lnb_ref, proj_ref, gatew_ref, og_ref, ob_ref, outw_ref,
+    act_ref, cot_ref, mask_ref, lng_ref, lnb_ref, proj_ref, gatew_ref, og_ref, ob_ref, outw_ref,
     pg_ref, recv_o,
-    xs, w_s, wo_s, vec_s, xf, wt_s, wot_s, gain_s, mask_s,
+    act_s, cot_s, mask_v, mask_sm, xs, w_s, wo_s, vec_s, xf, wt_s, wot_s, gain_s, mask_s,
     hat_s, inv_s, nrm_s, la_s, ga_s, lb_s, gb_s, go_s,
     mhat_s, minv_s, mn_s, oc_s, up_s, dout_s, dpre_s, acc_s,
-    scr_a, scr_b, lt_s, rt_s, dt_s,
+    dn_s, scr_a, scr_b, lt_s, rt_s, dt_s,
     send_lr, recv_lr, send_m, recv_m, send_d, recv_d, send_g, recv_g,
     pgb, gs, recv_b,
-    psend, precv, ssem, rsem, dsem,
+    isem, psend, precv, ssem, rsem, dsem,
 ):
     m, r, c = lax.axis_index("section"), lax.axis_index("row"), lax.axis_index("col")
     me = r * COLS + c
@@ -53,57 +53,76 @@
     def step4(v):
         return jnp.where(v == 0, 2, jnp.where(v == 3, 0, 2 * v - 1))
 
-    def peer(k):
-        to_r = lax.rem(r + step4(lax.rem(k, 4)), 4)
-        to_c = lax.rem(z + step4(k // 16), 4) * 4 + lax.rem(y + step4(lax.rem(k // 4, 4)), 4)
-        return to_r, to_c, to_r * COLS + to_c
+    def column(k):
+        return lax.rem(z + step4(k // 4), 4) * 4 + lax.rem(y + step4(lax.rem(k, 4)), 4)
+
+    def each_peer(visit, with_own_place):
+        def four(k, carry):
+            to_c = column(k)
+            for step in (2, 1, 3):
+                visit(lax.rem(r + step, 4), to_c)
+            if with_own_place:
+                visit(r, to_c)
+            else:
+                pl.when(k < COLS - 1)(lambda: visit(r, to_c))
+            return carry
+
+        lax.fori_loop(0, COLS, four, 0)
+
+    loads = [
+        pltpu.make_async_copy(src, dst, isem.at[n])
+        for n, (src, dst) in enumerate(
+            [
+                (act_ref.at[m], act_s.at[m]), (act_ref.at[other], act_s.at[other]), (cot_ref.at[m], cot_s),
+                (proj_ref, w_s.at[m, :, pl.ds(0, 512)]), (gatew_ref, w_s.at[m, :, pl.ds(512, 128)]), (outw_ref, wo_s.at[m]),
+                (lng_ref, vec_s.at[m, pl.ds(0, 1)]), (lnb_ref, vec_s.at[m, pl.ds(1, 1)]),
+                (og_ref, vec_s.at[m, pl.ds(2, 1)]), (ob_ref, vec_s.at[m, pl.ds(3, 1)]),
+                (mask_ref, mask_v), (mask_ref, mask_sm),
+            ]
+        )
+    ]
+    for load in loads:
+        load.start()
 
     barrier = pltpu.get_barrier_semaphore()
 
-    def greet(k, carry):
-        to_r, to_c, _ = peer(k)
-        pl.semaphore_signal(barrier, inc=1, device_id=(other, to_r, to_c), device_id_type=MESH)
-
-        @pl.when(k < PEERS - 1)
-        def _():
-            pl.semaphore_signal(barrier, inc=1, device_id=(m, to_r, to_c), device_id_type=MESH)
-
-        return carry
-
-    lax.fori_loop(0, PEERS, greet, 0)
+    def greet(core):
+        def visit(to_r, to_c):
+            pl.semaphore_signal(barrier, inc=1, device_id=(core, to_r, to_c), device_id_type=MESH)
+
+        return visit
+
+    each_peer(greet(m), False)
+    each_peer(greet(other), True)
+    for load in loads[3:] + loads[:2]:
+        load.wait()
+    vec_s[m, 4:8] = jnp.zeros((4, 128), F32)
 
     low = lax.broadcasted_iota(jnp.int32, (128, 128), 1) < 64
     low1 = lax.broadcasted_iota(jnp.int32, (8, 128), 1) < 64
 
     def exchange(src, dst, phase, sec):
-        def send(k, carry):
-            to_r, to_c, d = peer(k)
+        def send(to_r, to_c):
             pltpu.make_async_remote_copy(
-                src.at[sec, d], dst.at[sec, me], ssem.at[phase, sec], rsem.at[phase, sec],
+                src.at[sec, to_r * COLS + to_c], dst.at[sec, me], ssem.at[phase, sec], rsem.at[phase, sec],
                 device_id=(m, to_r, to_c), device_id_type=MESH,
             ).start()
-            return carry
-
-        lax.fori_loop(0, PEERS - 1, send, 0)
+
+        each_peer(send, False)
         dst[sec, me] = src[sec, me]
 
     def exchange_lr():
-        def send(k, carry):
-            to_r, to_c, d = peer(k)
-            for dest in (m, other):
-                def start(dest=dest):
-                    pltpu.make_async_remote_copy(
-                        send_lr.at[dest, d], recv_lr.at[m, me], ssem.at[LR, dest], rsem.at[LR, m],
-                        device_id=(dest, to_r, to_c), device_id_type=MESH,
-                    ).start()
-
-                if dest is m:
-                    pl.when(k < PEERS - 1)(start)
-                else:
-                    start()
-            return carry
-
-        lax.fori_loop(0, PEERS, send, 0)
+        def send(dest):
+            def visit(to_r, to_c):
+                pltpu.make_async_remote_copy(
+                    send_lr.at[dest, to_r * COLS + to_c], recv_lr.at[m, me], ssem.at[LR, dest], rsem.at[LR, m],
+                    device_id=(dest, to_r, to_c), device_id_type=MESH,
+                ).start()
+
+            return visit
+
+        each_peer(send(other), True)
+        each_peer(send(m), False)
         recv_lr[m, me] = send_lr[m, me]
 
     def arrived_lr(sec):
@@ -279,6 +298,54 @@
         send_d[sec] = scr_b[...].reshape(PEERS, 16, 128).astype(BF16)
         exchange(send_d, recv_d, DMIX, sec)
 
+    def out_before(sec):
+        def block(b, carry):
+            at = lanes(b)
+            dout = (up_s[sec, :, at] * go_s[sec, :, at]).astype(BF16)
+            dout_s[sec, :, at] = dout
+            dn_s[:, at] = dot(wo_s[sec], dout)
+            return carry
+
+        lax.fori_loop(0, 4, block, 0)
+
+    def out_chain(sec):
+        arrived(recv_m, MIX, sec)
+        scr_a[...] = recv_m[sec].astype(F32).reshape(N, 128)
+
+        def block(b, carry):
+            at = lanes(b)
+            x = gathered(scr_a, b)
+            centred = x - mean0(x)
+            inv = lax.rsqrt(mean0(centred * centred) + EPSILON)
+            hat = centred * inv
+            mhat_s[sec, :, at] = hat
+            e = dn_s[:, at] * wide(gain_s[sec, 2])
+            spread((e - mean0(e) - hat * mean0(e * hat)) * inv, scr_b, b)
+            return carry
+
+        lax.fori_loop(0, 4, block, 0)
+        send_d[sec] = scr_b[...].reshape(PEERS, 16, 128).astype(BF16)
+        exchange(send_d, recv_d, DMIX, sec)
+
+    def out_after(sec):
+        acc_s[sec, 2] = jnp.zeros((128, WIDE), F32)
+        acc_s[sec, 3] = jnp.zeros((128, WIDE), F32)
+
+        def block(b, carry):
+            at = lanes(b)
+            hat = mhat_s[sec, :, at]
+            mn = (hat * wide(gain_s[sec, 2]) + wide(gain_s[sec, 3])).astype(BF16)
+            mn_s[sec, :, at] = mn
+            gate = go_s[sec, :, at]
+            dgate = up_s[sec, :, at] * dot(wot_s[sec], mn) * gate * (1.0 - gate)
+            dpre_s[sec, 512:640, at] = dgate.astype(BF16)
+            dn = dn_s[:, at]
+            acc_s[sec, 2] += dn * hat
+            acc_s[sec, 3] += dn
+            return carry
+
+        lax.fori_loop(0, 4, block, 0)
+
     def products_back(sec):
         arrived(recv_d, DMIX, sec)
         assemble(recv_d, sec, 0, dt_s, 0)
@@ -345,26 +412,33 @@
         scatter_grads(sec, False)
 
     def scatter_grads(sec, early):
-        def send(k, carry):
-            to_r, to_c, d = peer(k)
-            in_early = jnp.logical_and(d >= 32, d < 48)
-            wanted = in_early if early else jnp.logical_and(d < OWNERS, jnp.logical_not(in_early))
-            away = jnp.logical_or(m != sec, k < PEERS - 1)
-
-            @pl.when(jnp.logical_and(wanted, away))
+        def give(to_r, to_c):
+            d = to_r * COLS + to_c
+            mine = jnp.logical_and(m == sec, d == me)
+
+            @pl.when(jnp.logical_not(mine))
             def _():
                 pltpu.make_async_remote_copy(
                     gs.at[sec, d], recv_b.at[m * PEERS + me], ssem.at[RS, sec], rsem.at[RS, 0],
                     device_id=(sec, to_r, to_c), device_id_type=MESH,
                 ).start()
 
-            @pl.when(jnp.logical_and(wanted, jnp.logical_not(away)))
+            @pl.when(mine)
             def _():
                 recv_b[m * PEERS + me] = gs[sec, d]
 
-            return carry
-
-        lax.fori_loop(0, PEERS, send, 0)
+        def send(k, carry):
+            to_c = column(k)
+            if early:
+                give(2, to_c)
+            else:
+                give(0, to_c)
+                give(1, to_c)
+            return carry
+
+        lax.fori_loop(0, COLS, send, 0)
+        if not early:
+            give(3, 0)
 
     def gather_grads():
         @pl.when(me < OWNERS)
@@ -373,29 +447,17 @@
             pltpu.make_async_copy(part, part, rsem.at[RS, 0]).wait()
             recv_o[me] = jnp.sum(recv_b[...].astype(F32), axis=0)
 
-            def give(k, carry):
-                to_r, to_c, _ = peer(k)
+            def give(to_r, to_c):
                 pltpu.make_async_remote_copy(
                     recv_o.at[me], recv_o.at[me], dsem.at[0], dsem.at[1],
                     device_id=(m, to_r, to_c), device_id_type=MESH,
                 ).start()
-                return carry
-
-            lax.fori_loop(0, PEERS - 1, give, 0)
-
-    xs[m] = act_ref[m]
-    w_s[m, :, 0:512] = proj_ref[...]
-    w_s[m, :, 512:640] = gatew_ref[...]
-    wo_s[m] = outw_ref[...]
-    vec_s[m, 0:1] = lng_ref[...]
-    vec_s[m, 1:2] = lnb_ref[...]
-    vec_s[m, 2:3] = og_ref[...]
-    vec_s[m, 3:4] = ob_ref[...]
-    vec_s[m, 4:8] = jnp.zeros((4, 128), F32)
+
+            each_peer(give, False)
 
     prepare(m)
-    front(m, act_ref.at[m], True, m)
-    front(m, act_ref.at[other], False, other)
+    front(m, act_s.at[m], True, m)
+    front(m, act_s.at[other], False, other)
     pl.semaphore_wait(barrier, 2 * PEERS - 1)
 
     @pl.when(m == 1)
@@ -407,21 +469,23 @@
             src, dst, psend.at[n], precv.at[n], device_id=partner, device_id_type=MESH
         )
         for n, (src, dst) in enumerate(
-            [(act_ref.at[other], xs.at[m]), (w_s.at[m], w_s.at[m]), (wo_s.at[m], wo_s.at[m]), (vec_s.at[m], vec_s.at[m])]
+            [(act_s.at[other], xs.at[m]), (w_s.at[m], w_s.at[m]), (wo_s.at[m], wo_s.at[m]), (vec_s.at[m], vec_s.at[m])]
         )
     ]
     for swap in swaps:
         swap.start()
 
     def turn(b, carry):
-        up_s[1, :, lanes(b)] = cells_to_lanes(cot_ref.at[m], b)
+        up_s[1, :, lanes(b)] = cells_to_lanes(cot_s, b)
         return carry
 
+    loads[2].wait()
     lax.fori_loop(0, 4, turn, 0)
     for swap in swaps:
         swap.wait_recv()
     prepare(other)
     front(other, xs.at[other], True, None)
+    out_before(1)
 
     mix(1)
 
@@ -429,9 +493,9 @@
     def _():
         exchange_lr()
 
-    out_forward(1)
-    out_backward(1)
+    out_chain(1)
     mix(0)
+    out_after(1)
     early_grads(1)
     products_back(1)
     out_forward(0)
@@ -454,10 +518,6 @@
     products_back(0)
     early_grads(0)
 
-    @pl.when(m == 1)
-    def _():
-        gather_grads()
-
     in_part(0)
     late_grads(0)
     back_to_cells(0)
@@ -469,7 +529,8 @@
     @pl.when(m == 0)
     def _():
         pg_ref[0] = pgb[0]
-        gather_grads()
+
+    gather_grads()
 
     for src, phase in ((send_m, MIX), (send_d, DMIX), (send_g, DLR)):
         for sec in range(2):
@@ -503,28 +564,31 @@
         pltpu.make_async_copy(part, part, dsem.at[0]).wait()
 
 
-def write_out(pg_in, o_ref, pg_ref, glng_ref, glnb_ref, gproj_ref, ggate_ref, gog_ref, gob_ref, gow_ref, held, sem_in, sem_out):
+def write_out(pg_in, o_in, pg_ref, glng_ref, glnb_ref, gproj_ref, ggate_ref, gog_ref, gob_ref, gow_ref, held, o_ref, sem_in, sem_out, sem_o):
+    rows = pltpu.make_async_copy(o_in.at[pl.ds(0, OWNERS)], o_ref, sem_o.at[0])
     parts = [pl.ds(n * 256, 256) for n in range(8)]
     come = [pltpu.make_async_copy(pg_in.at[p], held.at[p], sem_in.at[n]) for n, p in enumerate(parts)]
     go = [pltpu.make_async_copy(held.at[p], pg_ref.at[p], sem_out.at[n]) for n, p in enumerate(parts)]
     for copy in come:
         copy.start()
+    rows.start()
+    for copy_in, copy_out in zip(come, go):
+        copy_in.wait()
+        copy_out.start()
+    rows.wait()
     for o in range(4):
         gproj_ref[:, 128 * o:128 * o + 128] = o_ref[8 * o:8 * o + 8].reshape(128, 128)
     ggate_ref[...] = o_ref[32:40].reshape(128, 128)
     gow_ref[...] = o_ref[40:48].reshape(128, 128)
     for v, ref in enumerate((glng_ref, glnb_ref, gog_ref, gob_ref)):
         ref[...] = o_ref[48, v:v + 1, :] + o_ref[48, 8 + v:9 + v, :]
-    for copy_in, copy_out in zip(come, go):
-        copy_in.wait()
-        copy_out.start()
     for copy in go:
         copy.wait()
 
 
 def on_device(act, cot, mask, lng, lnb, proj, gatew, og, ob, outw):
     vmem = pl.BlockSpec(memory_space=pltpu.VMEM)
-    smem = pl.BlockSpec(memory_space=pltpu.SMEM)
+    anywhere = pl.BlockSpec(memory_space=pl.ANY)
 
     def v(shape, dtype=F32):
         return pltpu.VMEM(shape, dtype)
@@ -533,22 +597,23 @@
     pg, rows = pl.pallas_call(
         kernel,
         out_shape=(sds((2, N, 128), F32), sds((PEERS, 16, 128), F32)),
-        in_specs=[vmem, vmem, vmem, smem] + [vmem] * 7,
+        in_specs=[anywhere] * 10,
         out_specs=(vmem,) * 2,
         scratch_shapes=[
+            v((2, N, 128), BF16), v((N, 128)), v((2, 256), jnp.int32), pltpu.SMEM((2, 256), jnp.int32),
             v((2, N, 128), BF16), v((2, 128, 640), BF16), v((2, 128, 128), BF16), v((2, 8, 128)), v((N, 128)),
             v((2, 640, 128), BF16), v((2, 128, 128), BF16), v((2, 4, 128, 128)), v((2, 8, N)),
             v((2, 128, N)), v((2, 8, N)), v((2, 128, N), BF16),
             v((2, 128, N)), v((2, 128, N)), v((2, 128, N)), v((2, 128, N)), v((2, 128, N)),
             v((2, 128, N)), v((2, 8, N)), v((2, 128, N), BF16), v((2, 128, N)), v((3, 128, N)),
             v((2, 128, N), BF16), v((2, 640, N), BF16), v((2, 4, 128, WIDE)),
-            v((N, 128)), v((N, 128)), v((4, 256, 256), BF16), v((4, 256, 256), BF16), v((2, 256, 256), BF16),
+            v((128, N)), v((N, 128)), v((N, 128)), v((4, 256, 256), BF16), v((4, 256, 256), BF16), v((2, 256, 256), BF16),
             v((2, PEERS, 32, 128), BF16), v((2, PEERS, 32, 128), BF16),
             v((2, PEERS, 16, 128), BF16), v((2, PEERS, 16, 128), BF16),
             v((2, PEERS, 16, 128), BF16), v((2, PEERS, 16, 128), BF16),
             v((2, PEERS, 32, 128), BF16), v((2, PEERS, 32, 128), BF16),
             v((2, N, 128)), v((2, OWNERS, 16, 128), BF16), v((2 * PEERS, 16, 128), BF16),
-            pltpu.SemaphoreType.DMA((5,)), pltpu.SemaphoreType.DMA((5,)),
+            pltpu.SemaphoreType.DMA((12,)), pltpu.SemaphoreType.DMA((5,)), pltpu.SemaphoreType.DMA((5,)),
             pltpu.SemaphoreType.DMA((5, 2)), pltpu.SemaphoreType.DMA((5, 2)),
             pltpu.SemaphoreType.DMA((2,)),
         ],
@@ -556,18 +621,20 @@
             collective_id=1, has_side_effects=True, vmem_limit_bytes=56 * 2**20
         ),
     )(
-        act.reshape(2, N, 128), cot.reshape(2, N, 128), mask, mask, lng, lnb, proj[0], gatew[0], og, ob, outw[0]
+        act.reshape(2, N, 128), cot.reshape(2, N, 128), mask, lng, lnb, proj[0], gatew[0], og, ob, outw[0]
     )
-    anywhere = pl.BlockSpec(memory_space=pl.ANY)
     pg, glng, glnb, gproj, ggate, gog, gob, gow = pl.pallas_call(
         write_out,
         out_shape=(
             sds((2 * N, 128), F32), sds((1, 128), F32), sds((1, 128), F32), sds((128, 512), F32),
             sds((128, 128), F32), sds((1, 128), F32), sds((1, 128), F32), sds((128, 128), F32),
         ),
-        in_specs=[anywhere, vmem],
+        in_specs=[anywhere, anywhere],
         out_specs=(anywhere,) + (vmem,) * 7,
-        scratch_shapes=[v((2 * N, 128)), pltpu.SemaphoreType.DMA((8,)), pltpu.SemaphoreType.DMA((8,))],
+        scratch_shapes=[
+            v((2 * N, 128)), v((OWNERS, 16, 128)),
+            pltpu.SemaphoreType.DMA((8,)), pltpu.SemaphoreType.DMA((8,)), pltpu.SemaphoreType.DMA((1,)),
+        ],
     )(pg.reshape(2 * N, 128), rows)
     return (
         pg.reshape(1, 2, 64, 16, 128), glng, glnb, gproj[None], ggate[None], gog, gob, gow[None],

time: 93.7 us -> 84.2 us (0.90)
  Pallas kernels: 92.7 us -> 83.4 us
    pallas_call x1, Pallas kernels: 88.8 us -> 80.5 us  [on_device(): pl.pallas_call(kernel, out_shape=(sds((2, N, 128), F32), sds((PEERS, 16,...]
    pallas_call x1, Pallas kernels: 3.88 us -> 2.85 us  [on_device(): pl.pallas_call(write_out, out_shape=(sds((2 * N, 128), F32), sds((1, 128)...]
where the time goes in v3:
time: 84.2 us; the launch traced here: 84 us
  Pallas kernels  83.4 us (99%)
    pallas_call x1, Pallas kernels, on_device(): pl.pallas_call(kernel, out_shape=(sds((2, N, 128), F32), sds((PEERS, 16,...  80.5 us
    pallas_call x1, Pallas kernels, on_device(): pl.pallas_call(write_out, out_shape=(sds((2 * N, 128), F32), sds((1, 128)...  2.85 us

profile of v3, /device:TPU:0, one launch (start us, length us, event | category | flops | bytes accessed | tf_op | source)
XLA Modules:
  0.0 84.0 jit_solution(6351735282578431375)
XLA Ops:
  0.6 80.5 %shard_map.161 = (f32[2,1024,128]{2,1,0:T(8,128)}, f32[64,16,128]{2,1,0:T(8,128)}) custom-call(bf16[2,1024,128]{2,1,0:T(8,128)(2,1)} %bitcast.12, f32[2,1024,128]{2,1,0:T(8,128)} %bitcast.10, s32[2,256]{1,0:T(2,128)} %mask_ref.1, f32[1,128]{1,0:T(1,128)} %lng_ref.1, f32[1,128]{1,0:T(1,128)} %lnb_ref.1, bf16[128,512]{1,0:T(8,128)(2,1)} %bitcast.13, ...), custom_call_target="tpu_custom_call" | custom-call | tf_op jit(solution)/shard_map/pallas_call | solution.py:597
  81.2 2.9 %shard_map.162 = (f32[2048,128]{1,0:T(8,128)}, f32[1,128]{1,0:T(1,128)}, f32[1,128]{1,0:T(1,128)}, f32[128,512]{1,0:T(8,128)}, f32[128,128]{1,0:T(8,128)}, /*ind...) custom-call(f32[2048,128]{1,0:T(8,128)} %bitcast.11, f32[64,16,128]{2,1,0:T(8,128)} %get-tuple-element.19.o_in), custom_call_target="tpu_custom_call" | custom-call | tf_op jit(solution)/shard_map/pallas_call | solution.py:626

commit v4 on v3

--- a/solution.py
+++ b/solution.py
@@ -81,9 +81,6 @@
             ]
         )
     ]
-    for load in loads:
-        load.start()
-
     barrier = pltpu.get_barrier_semaphore()
 
     def greet(core):
@@ -92,9 +89,20 @@
 
         return visit
 
-    each_peer(greet(m), False)
-    each_peer(greet(other), True)
-    for load in loads[3:] + loads[:2]:
+    @pl.when(m == 0)
+    def _():
+        each_peer(greet(other), True)
+        each_peer(greet(m), False)
+
+    @pl.when(m == 1)
+    def _():
+        each_peer(greet(m), False)
+        each_peer(greet(other), True)
+
+    for load in loads:
+        load.start()
+
+    for load in loads[3:]:
         load.wait()
     vec_s[m, 4:8] = jnp.zeros((4, 128), F32)
 
@@ -111,7 +119,7 @@
         each_peer(send, False)
         dst[sec, me] = src[sec, me]
 
-    def exchange_lr():
+    def exchange_lr(to_other=True, to_own=True):
         def send(dest):
             def visit(to_r, to_c):
                 pltpu.make_async_remote_copy(
@@ -121,9 +129,11 @@
 
             return visit
 
-        each_peer(send(other), True)
-        each_peer(send(m), False)
-        recv_lr[m, me] = send_lr[m, me]
+        if to_other:
+            each_peer(send(other), True)
+        if to_own:
+            each_peer(send(m), False)
+            recv_lr[m, me] = send_lr[m, me]
 
     def arrived_lr(sec):
         @pl.when(m == sec)
@@ -276,27 +286,32 @@
         lax.fori_loop(0, 4, block, 0)
 
     def out_backward(sec):
+        def block(b, carry):
+            at = lanes(b)
+            dout = (up_s[sec, :, at] * go_s[sec, :, at]).astype(BF16)
+            dout_s[sec, :, at] = dout
+            dn = dot(wo_s[sec], dout)
+            dn_s[:, at] = dn
+            hat = mhat_s[sec, :, at]
+            e = dn * wide(gain_s[sec, 2])
+            spread((e - mean0(e) - hat * mean0(e * hat)) * minv_s[sec, 0:1, at], scr_b, b)
+            return carry
+
+        lax.fori_loop(0, 4, block, 0)
+        send_d[sec] = scr_b[...].reshape(PEERS, 16, 128).astype(BF16)
+        exchange(send_d, recv_d, DMIX, sec)
         acc_s[sec, 2] = jnp.zeros((128, WIDE), F32)
         acc_s[sec, 3] = jnp.zeros((128, WIDE), F32)
 
-        def block(b, carry):
-            at = lanes(b)
-            up = up_s[sec, :, at]
-            dout = (up * go_s[sec, :, at]).astype(BF16)
-            dout_s[sec, :, at] = dout
-            dpre_s[sec, 512:640, at] = (up * oc_s[sec, :, at]).astype(BF16)
-            dn = dot(wo_s[sec], dout)
-            hat = mhat_s[sec, :, at]
-            acc_s[sec, 2] += dn * hat
+        def rest(b, carry):
+            at = lanes(b)
+            dpre_s[sec, 512:640, at] = (up_s[sec, :, at] * oc_s[sec, :, at]).astype(BF16)
+            dn = dn_s[:, at]
+            acc_s[sec, 2] += dn * mhat_s[sec, :, at]
             acc_s[sec, 3] += dn
-            e = dn * wide(gain_s[sec, 2])
-            d = (e - mean0(e) - hat * mean0(e * hat)) * minv_s[sec, 0:1, at]
-            spread(d, scr_b, b)
-            return carry
-
-        lax.fori_loop(0, 4, block, 0)
-        send_d[sec] = scr_b[...].reshape(PEERS, 16, 128).astype(BF16)
-        exchange(send_d, recv_d, DMIX, sec)
+            return carry
+
+        lax.fori_loop(0, 4, rest, 0)
 
     def out_before(sec):
         def block(b, carry):
@@ -445,7 +460,11 @@
         def _():
             part = recv_b.at[pl.ds(0, 2 * PEERS - 1)]
             pltpu.make_async_copy(part, part, rsem.at[RS, 0]).wait()
-            recv_o[me] = jnp.sum(recv_b[...].astype(F32), axis=0)
+            total = jnp.sum(recv_b[...].astype(F32), axis=0)
+            vectors = total[0:8] + total[8:16]
+            high = vectors.astype(BF16).astype(F32)
+            split = jnp.concatenate([high, vectors - high], axis=0)
+            recv_o[me] = jnp.where(me == OWNERS - 1, split, total).astype(BF16)
 
             def give(to_r, to_c):
                 pltpu.make_async_remote_copy(
@@ -456,13 +475,14 @@
             each_peer(give, False)
 
     prepare(m)
-    front(m, act_s.at[m], True, m)
+    loads[1].wait()
     front(m, act_s.at[other], False, other)
+    loads[0].wait()
     pl.semaphore_wait(barrier, 2 * PEERS - 1)
 
     @pl.when(m == 1)
     def _():
-        exchange_lr()
+        exchange_lr(to_own=False)
 
     swaps = [
         pltpu.make_async_remote_copy(
@@ -475,6 +495,12 @@
     for swap in swaps:
         swap.start()
 
+    front(m, act_s.at[m], True, m)
+
+    @pl.when(m == 1)
+    def _():
+        exchange_lr(to_other=False)
+
     def turn(b, carry):
         up_s[1, :, lanes(b)] = cells_to_lanes(cot_s, b)
         return carry
@@ -495,14 +521,15 @@
 
     out_chain(1)
     mix(0)
+    products_back(1)
     out_after(1)
-    early_grads(1)
-    products_back(1)
     out_forward(0)
     in_part(1)
     out_backward(0)
+    early_grads(1)
     late_grads(1)
     back_to_cells(1)
+    kept = pltpu.make_async_copy(pgb.at[m], pg_ref.at[m], dsem.at[2])
     handed = pltpu.make_async_remote_copy(
         pgb.at[other], pg_ref.at[m], psend.at[PG_COPY], precv.at[PG_COPY], device_id=partner, device_id_type=MESH
     )
@@ -513,7 +540,7 @@
 
     @pl.when(m == 1)
     def _():
-        pg_ref[1] = pgb[1]
+        kept.start()
 
     products_back(0)
     early_grads(0)
@@ -528,7 +555,7 @@
 
     @pl.when(m == 0)
     def _():
-        pg_ref[0] = pgb[0]
+        kept.start()
 
     gather_grads()
 
@@ -550,6 +577,7 @@
     for swap in swaps:
         swap.wait_send()
     handed.wait()
+    kept.wait()
 
     @pl.when(me >= OWNERS)
     def _():
@@ -577,11 +605,12 @@
         copy_out.start()
     rows.wait()
     for o in range(4):
-        gproj_ref[:, 128 * o:128 * o + 128] = o_ref[8 * o:8 * o + 8].reshape(128, 128)
-    ggate_ref[...] = o_ref[32:40].reshape(128, 128)
-    gow_ref[...] = o_ref[40:48].reshape(128, 128)
+        gproj_ref[:, 128 * o:128 * o + 128] = o_ref[8 * o:8 * o + 8].astype(F32).reshape(128, 128)
+    ggate_ref[...] = o_ref[32:40].astype(F32).reshape(128, 128)
+    gow_ref[...] = o_ref[40:48].astype(F32).reshape(128, 128)
+    vectors = o_ref[48].astype(F32)
     for v, ref in enumerate((glng_ref, glnb_ref, gog_ref, gob_ref)):
-        ref[...] = o_ref[48, v:v + 1, :] + o_ref[48, 8 + v:9 + v, :]
+        ref[...] = vectors[v:v + 1] + vectors[8 + v:9 + v]
     for copy in go:
         copy.wait()
 
@@ -596,9 +625,9 @@
     sds = jax.ShapeDtypeStruct
     pg, rows = pl.pallas_call(
         kernel,
-        out_shape=(sds((2, N, 128), F32), sds((PEERS, 16, 128), F32)),
+        out_shape=(sds((2, N, 128), F32), sds((PEERS, 16, 128), BF16)),
         in_specs=[anywhere] * 10,
-        out_specs=(vmem,) * 2,
+        out_specs=(anywhere, vmem),
         scratch_shapes=[
             v((2, N, 128), BF16), v((N, 128)), v((2, 256), jnp.int32), pltpu.SMEM((2, 256), jnp.int32),
             v((2, N, 128), BF16), v((2, 128, 640), BF16), v((2, 128, 128), BF16), v((2, 8, 128)), v((N, 128)),
@@ -615,7 +644,7 @@
             v((2, N, 128)), v((2, OWNERS, 16, 128), BF16), v((2 * PEERS, 16, 128), BF16),
             pltpu.SemaphoreType.DMA((12,)), pltpu.SemaphoreType.DMA((5,)), pltpu.SemaphoreType.DMA((5,)),
             pltpu.SemaphoreType.DMA((5, 2)), pltpu.SemaphoreType.DMA((5, 2)),
-            pltpu.SemaphoreType.DMA((2,)),
+            pltpu.SemaphoreType.DMA((3,)),
         ],
         compiler_params=pltpu.CompilerParams(
             collective_id=1, has_side_effects=True, vmem_limit_bytes=56 * 2**20
@@ -632,7 +661,7 @@
         in_specs=[anywhere, anywhere],
         out_specs=(anywhere,) + (vmem,) * 7,
         scratch_shapes=[
-            v((2 * N, 128)), v((OWNERS, 16, 128)),
+            v((2 * N, 128)), v((OWNERS, 16, 128), BF16),
             pltpu.SemaphoreType.DMA((8,)), pltpu.SemaphoreType.DMA((8,)), pltpu.SemaphoreType.DMA((1,)),
         ],
     )(pg.reshape(2 * N, 128), rows)

time: 84.2 us -> 79.1 us (0.939)
  Pallas kernels: 83.4 us -> 78.3 us
    pallas_call x1, Pallas kernels: 80.5 us -> 75.5 us  [on_device(): pl.pallas_call(kernel, out_shape=(sds((2, N, 128), F32), sds((PEERS, 16,...]
where the time goes in v4:
time: 79.1 us; the launch traced here: 79 us
  Pallas kernels  78.3 us (99%)
    pallas_call x1, Pallas kernels, on_device(): pl.pallas_call(kernel, out_shape=(sds((2, N, 128), F32), sds((PEERS, 16,...  75.5 us
    pallas_call x1, Pallas kernels, on_device(): pl.pallas_call(write_out, out_shape=(sds((2 * N, 128), F32), sds((1, 128)...  2.85 us

profile of v4, /device:TPU:0, one launch (start us, length us, event | category | flops | bytes accessed | tf_op | source)
XLA Modules:
  0.0 79.0 jit_solution(4717931905110088753)
XLA Ops:
  0.6 75.5 %shard_map.161 = (f32[2,1024,128]{2,1,0:T(8,128)}, bf16[64,16,128]{2,1,0:T(8,128)(2,1)}) custom-call(bf16[2,1024,128]{2,1,0:T(8,128)(2,1)} %bitcast.12, f32[2,1024,128]{2,1,0:T(8,128)} %bitcast.10, s32[2,256]{1,0:T(2,128)} %mask_ref.1, f32[1,128]{1,0:T(1,128)} %lng_ref.1, f32[1,128]{1,0:T(1,128)} %lnb_ref.1, bf16[128,512]{1,0:T(8,128)(2,1)} %bitcast.13, ...), custom_call_target="tpu_custom_call" | custom-call | tf_op jit(solution)/shard_map/pallas_call | solution.py:626
  76.1 2.9 %shard_map.162 = (f32[2048,128]{1,0:T(8,128)}, f32[1,128]{1,0:T(1,128)}, f32[1,128]{1,0:T(1,128)}, f32[128,512]{1,0:T(8,128)}, f32[128,128]{1,0:T(8,128)}, /*ind...) custom-call(f32[2048,128]{1,0:T(8,128)} %bitcast.11, bf16[64,16,128]{2,1,0:T(8,128)(2,1)} %get-tuple-element.19.o_in), custom_call_target="tpu_custom_call" | custom-call | tf_op jit(solution)/shard_map/pallas_call | solution.py:655

commit v5 on v4

--- a/solution.py
+++ b/solution.py
@@ -517,7 +517,8 @@
 
     @pl.when(m == 0)
     def _():
-        exchange_lr()
+        exchange_lr(to_other=False)
+        exchange_lr(to_own=False)
 
     out_chain(1)
     mix(0)
@@ -528,6 +529,8 @@
     out_backward(0)
     early_grads(1)
     late_grads(1)
+    early_grads(0)
+    products_back(0)
     back_to_cells(1)
     kept = pltpu.make_async_copy(pgb.at[m], pg_ref.at[m], dsem.at[2])
     handed = pltpu.make_async_remote_copy(
@@ -542,8 +545,6 @@
     def _():
         kept.start()
 
-    products_back(0)
-    early_grads(0)
 
     in_part(0)
     late_grads(0)

time: 79.1 us -> 77.5 us (0.980)
  Pallas kernels: 78.3 us -> 76.7 us
    pallas_call x1, Pallas kernels: 75.5 us -> 73.8 us  [on_device(): pl.pallas_call(kernel, out_shape=(sds((2, N, 128), F32), sds((PEERS, 16,...]
where the time goes in v5:
time: 77.5 us; the launch traced here: 77.3 us
  Pallas kernels  76.7 us (99%)
    pallas_call x1, Pallas kernels, on_device(): pl.pallas_call(kernel, out_shape=(sds((2, N, 128), F32), sds((PEERS, 16,...  73.8 us
    pallas_call x1, Pallas kernels, on_device(): pl.pallas_call(write_out, out_shape=(sds((2 * N, 128), F32), sds((1, 128)...  2.85 us

profile of v5, /device:TPU:0, one launch (start us, length us, event | category | flops | bytes accessed | tf_op | source)
XLA Modules:
  0.0 77.3 jit_solution(17356976561242079863)
XLA Ops:
  0.6 73.8 %shard_map.161 = (f32[2,1024,128]{2,1,0:T(8,128)}, bf16[64,16,128]{2,1,0:T(8,128)(2,1)}) custom-call(bf16[2,1024,128]{2,1,0:T(8,128)(2,1)} %bitcast.12, f32[2,1024,128]{2,1,0:T(8,128)} %bitcast.10, s32[2,256]{1,0:T(2,128)} %mask_ref.1, f32[1,128]{1,0:T(1,128)} %lng_ref.1, f32[1,128]{1,0:T(1,128)} %lnb_ref.1, bf16[128,512]{1,0:T(8,128)(2,1)} %bitcast.13, ...), custom_call_target="tpu_custom_call" | custom-call | tf_op jit(solution)/shard_map/pallas_call | solution.py:627
  74.5 2.9 %shard_map.162 = (f32[2048,128]{1,0:T(8,128)}, f32[1,128]{1,0:T(1,128)}, f32[1,128]{1,0:T(1,128)}, f32[128,512]{1,0:T(8,128)}, f32[128,128]{1,0:T(8,128)}, /*ind...) custom-call(f32[2048,128]{1,0:T(8,128)} %bitcast.11, bf16[64,16,128]{2,1,0:T(8,128)(2,1)} %get-tuple-element.19.o_in), custom_call_target="tpu_custom_call" | custom-call | tf_op jit(solution)/shard_map/pallas_call | solution.py:656
